TPU v7x, 128 devices: a whole 4x4x4 slice. The times are simulated.
128 devices in a mesh: dp: 8 (over x_lo, y), fsdp: 16 (over x_hi, z, core).
Axes of the slice: x: 4 (x_hi: 2, x_lo: 2; x = x_hi * 2 + x_lo), y: 4, z: 4, core: 2. Of those that a mesh axis runs over, the one named last changes fastest.
Arguments:
- grads: bfloat16 [3, 2, 5120, 13824], P(None, None, 'dp', 'fsdp'), may hold values from -6 to 6
- basis_in: float32 [3, 2, 8, 5120, 128], P(None, None, 'dp', 'fsdp'), may hold values from -0.5 to 0.5
- eig_in: float32 [3, 2, 8, 5120], P(None, None, 'dp', 'fsdp'), may hold values from 0.3 to 3
- basis_out: float32 [3, 2, 8, 13824, 288], P(None, None, 'dp', 'fsdp'), may hold values from -0.375 to 0.375
- eig_out: float32 [3, 2, 8, 13824], P(None, None, 'dp', 'fsdp'), may hold values from 0.3 to 3
- owner: int32 [3, 2], replicated, may hold values from 0 to 7
Outputs:
- preconditioned: bfloat16 [3, 2, 5120, 13824], P(None, None, 'dp', 'fsdp')
All inputs are finite; a program needn't handle non-finite values.
Results may differ from a plain program's by a relative error of at most 0.001.
Values sent between devices are 32-bit elements; how exact they have to be, the bound alone decides.
No kernel may reach another device: no remote copies, remote signals or barrier semaphores. Data moves between devices by JAX's collectives and lax.ppermute only.
A program may use at most 128 MiB of HBM per device.

v0:
```python
import functools

import jax
import jax.numpy as jnp
from jax import lax
from jax.experimental import pallas as pl
from jax.experimental.pallas import tpu as pltpu
from jax.sharding import PartitionSpec as P

BI = 128
BO = 288
M = 6
damping = 0.1
PARAMS = pltpu.CompilerParams(vmem_limit_bytes=62 * 2**20)
F32 = jnp.float32
BF16 = jnp.bfloat16

PIECE = 48
WIDE = 896
HALF = 3 * PIECE
IN_ROWS = 336
PARTS = 3

BITS = (lambda v: v >> 2, lambda v: (v ^ (v >> 1)) & 1, lambda v: (v & 3) >> 1)
SWAPS = (lambda v: v ^ 4, lambda v: v ^ 1, lambda v: (v & 4) | (3 - (v & 3)))


def split(x):
    high = x.astype(BF16)
    return high, (x - high.astype(F32)).astype(BF16)


def dot(a, b):
    return jnp.dot(a, b, preferred_element_type=F32)


def dot_tn(a, b):
    return lax.dot_general(a, b, (((0,), (0,)), ((), ())), preferred_element_type=F32)


def block(*shape):
    return pl.BlockSpec((1, *shape), lambda m, *_: (m,) + (0,) * len(shape))


CHAINS = ((0, 0), (1, 0), (2, 0), (0, 1))
LIST = 7
THIRD = 2 * M
CHAIN = THIRD + 2 * LIST
OWN = len(CHAINS) * CHAIN
SIDE = OWN + LIST
CORE = SIDE + 3
TABLE = CORE + 1
SIZES = ((2, 5), (3, M), (M, M))


def table_kernel(owner_ref, out_ref, tier_ref):
    def clear(i, carry):
        out_ref[i] = 0
        return carry

    lax.fori_loop(0, TABLE, clear, 0)
    owners = [owner_ref[m % 2, m // 2] for m in range(M)]
    corner = [[BITS[d](v) for v in owners] for d in range(3)]
    at, over = lax.axis_index("dp"), lax.axis_index("fsdp")
    row = [BITS[d](at) for d in range(3)]
    column = [BITS[d](over >> 1) for d in range(3)]
    for c, (turn, axis) in enumerate(CHAINS):
        seen = [jnp.int32(0)] * 5
        spot = jnp.int32(0)
        for m in range(M):
            away = [corner[(turn + e) % 3][m] ^ row[(turn + e) % 3] for e in range(3)]
            if axis:
                away = [away[e] ^ column[(turn + e) % 3] for e in range(3)]
            array = jnp.where(away[2] == 1, 4, away[0] + 2 * away[1])
            slot = seen[0]
            for k in range(1, 5):
                slot = jnp.where(array == k, seen[k], slot)
            seen = [seen[k] + (array == k).astype(jnp.int32) for k in range(5)]
            out_ref[c * CHAIN + m] = array
            out_ref[c * CHAIN + M + m] = slot
            here = jnp.where(array < 4, spot, LIST - 1)
            out_ref[c * CHAIN + THIRD + here] = array
            out_ref[c * CHAIN + THIRD + LIST + here] = slot
            spot = spot + (array < 4).astype(jnp.int32)
            if c == 0:
                out_ref[OWN + jnp.where(array == 0, slot, LIST - 1)] = m
    for d in range(3):
        out_ref[SIDE + d] = row[d]
    node, face = jnp.int32(0), jnp.int32(0)
    for m in range(M):
        same = [[(corner[d][m] == corner[d][n]).astype(jnp.int32) for n in range(M)] for d in range(3)]
        node = jnp.maximum(node, sum(same[0][n] * same[1][n] * same[2][n] for n in range(M)))
        for d in range(3):
            face = jnp.maximum(face, sum(same[d]))
    tier = jnp.int32(len(SIZES) - 1)
    for k in range(len(SIZES) - 2, -1, -1):
        tier = jnp.where((node <= SIZES[k][0]) & (face <= SIZES[k][1]), k, tier)
    out_ref[CORE] = over & 1
    tier_ref[0] = tier


def make_tables(owner):
    smem = pl.BlockSpec(memory_space=pltpu.SMEM)
    return pl.pallas_call(
        table_kernel,
        out_shape=[jax.ShapeDtypeStruct((n,), jnp.int32) for n in (TABLE, 1)],
        in_specs=[smem],
        out_specs=[smem, smem],
        name="tables",
    )(owner)


HALVES = [(t, other) for other in (True, False) for t in range(3)]


def pack_kernel(table_ref, *refs):
    columns = refs[13]
    row = jnp.concatenate([refs[6][0, 0], jnp.zeros((1, 32), F32)], axis=1)
    lines = [row] + [pltpu.roll(row, WIDE - BO * o, 1) for o in (1, 2)]
    columns[...] = jnp.concatenate([x[:, 0:384] for x in lines] + [jnp.zeros((5, 384), F32)], axis=0).T
    for k, (t, other) in enumerate(HALVES):
        side = table_ref[SIDE + t]
        start = 2 * PIECE * t + PIECE * (1 - side if other else side)
        refs[7 + k][0, :, 0:864] = refs[k][0]
        refs[7 + k][0, :, 864:872] = columns[pl.ds(pl.multiple_of(start, PIECE), PIECE), :]
        refs[7 + k][0, :, 872:WIDE] = jnp.zeros((PIECE, 24), F32)


def pack(table, basis, eig, slots):
    def rows(t, other):
        def place(j, table):
            side = table[SIDE + t]
            return table[OWN + j], 2 * t + (1 - side if other else side), 0

        return pl.BlockSpec((1, PIECE, 864), place)

    out = pl.pallas_call(
        pack_kernel,
        out_shape=[jax.ShapeDtypeStruct((slots, PIECE, WIDE), F32)] * 6,
        grid_spec=pltpu.PrefetchScalarGridSpec(
            num_scalar_prefetch=1,
            grid=(slots,),
            in_specs=[rows(*half) for half in HALVES]
            + [pl.BlockSpec((1, 1, 1, 864), lambda j, table: (table[OWN + j] // 2, table[OWN + j] % 2, 0, 0))],
            out_specs=[block(PIECE, WIDE)] * 6,
            scratch_shapes=[pltpu.VMEM((384, 8), F32)],
        ),
        cost_estimate=pl.CostEstimate(flops=0, bytes_accessed=2_000_000 * slots, transcendentals=0),
        name="pack",
    )(table, *[basis] * 6, eig)
    return out[:3], out[3:]


ANY = pl.BlockSpec(memory_space=pl.ANY)
SMEM = pl.BlockSpec(memory_space=pltpu.SMEM)
VMEM = pl.BlockSpec(memory_space=pltpu.VMEM)


def gather_kernel(slots, table_ref, basis_ref, eig_ref, out_ref, sems):
    copies = []
    for j in range(slots):
        copies.append(pltpu.make_async_copy(basis_ref.at[table_ref[OWN + j]], out_ref.at[j, pl.ds(0, 320)], sems.at[j]))
    for copy in copies:
        copy.start()
    for j in range(slots):
        m = table_ref[OWN + j]
        line = jnp.concatenate([eig_ref[m // 2, m % 2], jnp.zeros((1, 64), F32)], axis=1)
        line = jnp.where(table_ref[CORE] == 0, line, pltpu.roll(line, 64, 1))
        rows = [line[:, 128 * k : 128 * (k + 1)] for k in range(3)]
        out_ref[j, 320:IN_ROWS, :] = jnp.concatenate(rows + [jnp.zeros((13, 128), F32)], axis=0)
    for copy in copies:
        copy.wait()


def gather_own(table, basis, eig, slots):
    return pl.pallas_call(
        functools.partial(gather_kernel, slots),
        out_shape=jax.ShapeDtypeStruct((slots, IN_ROWS, 128), F32),
        in_specs=[SMEM, ANY, VMEM],
        out_specs=VMEM,
        scratch_shapes=[pltpu.SemaphoreType.DMA((slots,))],
        cost_estimate=pl.CostEstimate(flops=0, bytes_accessed=400_000 * slots, transcendentals=0),
        name="gather",
    )(table, basis, eig)


def route_kernel(chains, slots, count, parts, table_ref, *refs):
    sources, outs, sems = refs[: count * len(chains)], refs[count * len(chains) : -1], refs[-1]
    each = slots // parts
    for i, c in enumerate(chains):
        for j in range(slots):
            base = c * CHAIN + (THIRD + j if count == 4 else j)
            array, slot = table_ref[base], table_ref[base + (LIST if count == 4 else M)]
            for k in range(count):

                @pl.when(array == k)
                def _():
                    out = outs[parts * i + j // each].at[j % each]
                    pltpu.make_async_copy(sources[count * i + k].at[slot], out, sems.at[i * slots + j]).start()

    for i in range(len(chains)):
        for j in range(slots):
            out = outs[parts * i + j // each].at[j % each]
            pltpu.make_async_copy(out, out, sems.at[i * slots + j]).wait()


def route(table, chains, slots, sources, shape, parts=1):
    count = len(sources[0])
    flat = [x for chain in sources for x in chain]
    return pl.pallas_call(
        functools.partial(route_kernel, chains, slots, count, parts),
        out_shape=[jax.ShapeDtypeStruct((slots // parts, *shape), F32)] * (parts * len(chains)),
        in_specs=[SMEM] + [ANY] * len(flat),
        out_specs=[VMEM] * (parts * len(chains)),
        scratch_shapes=[pltpu.SemaphoreType.DMA((len(chains) * slots,))],
        cost_estimate=pl.CostEstimate(flops=0, bytes_accessed=400_000 * slots, transcendentals=0),
        name="route",
    )(table, *flat)


def join_left(table_ref, mine, other, whole, a_scratch):
    core = table_ref[CORE]
    for k in range(PARTS):

        @pl.when(pl.program_id(0) // (M // PARTS) == k)
        def _():
            for half, at in ((mine, core), (other, 1 - core)):
                whole[pl.ds(pl.multiple_of(320 * at, 8), 320), :] = half[k][0, 0:320]
            low = jnp.where(core == 0, mine[k][0, 320:328], other[k][0, 320:328])
            high = jnp.where(core == 0, other[k][0, 320:328], mine[k][0, 320:328])
            a_scratch[0:2, :] = low[0:2]
            a_scratch[2:3, :] = low[2:3] + high[0:1]
            a_scratch[3:5, :] = high[1:3]


def doubled(value):
    high, low = split(value)
    both = jnp.concatenate([high, low], axis=1)
    return jnp.concatenate([both, both], axis=0)


def half_chain(grad_ref, pieces, whole, a_scratch, basis, turned, back, scaled):
    eigs = []
    for o in range(3):
        window = jnp.concatenate([ref[0, :, 256 * o : 256 * o + 384] for ref in pieces], axis=0)
        if o:
            window = pltpu.roll(window, 384 - 32 * o, 1)
        high, low = split(window[:, 0:BO])
        basis[o, 0:HALF, :] = high
        basis[o, HALF : 2 * HALF, :] = low
        back[o, 0:HALF, :] = high
        back[o, HALF : 2 * HALF, :] = high
        back[o, 2 * HALF : 3 * HALF, :] = low
        eigs.append(jnp.concatenate([ref[0, :, 768:WIDE][:, 96 + o : 97 + o] for ref in pieces], axis=0))

    for o in range(3):
        product = dot(basis[o], grad_ref[0, BO * o : BO * (o + 1), :])
        high, low = split(product[0:HALF] + product[HALF : 2 * HALF])
        for i in range(5):
            turned[i, HALF * o : HALF * (o + 1), 0:128] = high[:, BI * i : BI * (i + 1)]
            turned[i, HALF * o : HALF * (o + 1), 128:256] = low[:, BI * i : BI * (i + 1)]

    for i in range(5):
        product = dot(turned[i], doubled(whole[BI * i : BI * (i + 1), :]))
        rotated = product[:, 0:128] + product[:, 128:256]
        columns = slice(BI * i, BI * (i + 1))
        for o in range(3):
            part = rotated[HALF * o : HALF * (o + 1)] / (eigs[o] * a_scratch[i : i + 1, :] + damping)
            high, low = split(part)
            scaled[o, 0:HALF, columns] = high
            scaled[o, HALF : 2 * HALF, columns] = low
            scaled[o, 2 * HALF : 3 * HALF, columns] = high

    for o in range(3):
        yield o, dot_tn(back[o], scaled[o])


def mine_kernel(table_ref, grad_ref, p0, p1, p2, *refs):
    left, across, (out_ref, *scratch) = refs[:PARTS], refs[PARTS : 2 * PARTS], refs[2 * PARTS :]
    join_left(table_ref, left, across, *scratch[:2])
    for o, value in half_chain(grad_ref, (p0, p1, p2), *scratch):
        out_ref[0, BO * o : BO * (o + 1), :] = value


def other_kernel(table_ref, grad_ref, p0, p1, p2, *refs):
    left, across, (part_ref, out_ref, *scratch, whole) = refs[:PARTS], refs[PARTS : 2 * PARTS], refs[2 * PARTS :]
    join_left(table_ref, left, across, *scratch[:2])
    for o, value in half_chain(grad_ref, (p0, p1, p2), *scratch):
        rows = slice(BO * o, BO * (o + 1))
        high, low = split(value + part_ref[0, rows, :])
        for i in range(5):
            whole[i, rows, 0:128] = high[:, BI * i : BI * (i + 1)]
            whole[i, rows, 128:256] = low[:, BI * i : BI * (i + 1)]
    for i in range(5):
        product = dot(whole[i], doubled(scratch[0][BI * i : BI * (i + 1), :].T))
        out_ref[0, :, BI * i : BI * (i + 1)] = (product[:, 0:128] + product[:, 128:256]).astype(BF16)


CHAIN_SCRATCH = [
    pltpu.VMEM((640, 128), F32),
    pltpu.VMEM((8, 128), F32),
    pltpu.VMEM((3, 2 * HALF, BO), BF16),
    pltpu.VMEM((5, 3 * HALF, 256), BF16),
    pltpu.VMEM((3, 3 * HALF, BO), BF16),
    pltpu.VMEM((3, 3 * HALF, 640), BF16),
]
def part_block(k):
    each = M // PARTS
    return pl.BlockSpec((1, IN_ROWS, 128), lambda m, *_: (jnp.clip(m - each * k, 0, each - 1), 0, 0))


CHAIN_IN = [block(864, 640)] + [block(PIECE, WIDE)] * 3 + [part_block(k) for k in range(PARTS)] * 2


def chain_mine(table, grads, pieces, left):
    return pl.pallas_call(
        mine_kernel,
        out_shape=jax.ShapeDtypeStruct((M, 864, 640), F32),
        grid_spec=pltpu.PrefetchScalarGridSpec(
            num_scalar_prefetch=1,
            grid=(M,),
            in_specs=CHAIN_IN,
            out_specs=block(864, 640),
            scratch_shapes=CHAIN_SCRATCH,
        ),
        compiler_params=PARAMS,
        cost_estimate=pl.CostEstimate(flops=1_000_000, bytes_accessed=1_000_000, transcendentals=0),
        name="mine",
    )(table, grads, *pieces, *left)


def chain_other(table, grads, pieces, left, part):
    return pl.pallas_call(
        other_kernel,
        out_shape=jax.ShapeDtypeStruct((M, 864, 640), BF16),
        grid_spec=pltpu.PrefetchScalarGridSpec(
            num_scalar_prefetch=1,
            grid=(M,),
            in_specs=CHAIN_IN + [block(864, 640)],
            out_specs=block(864, 640),
            scratch_shapes=CHAIN_SCRATCH + [pltpu.VMEM((5, 864, 256), BF16)],
        ),
        compiler_params=PARAMS,
        cost_estimate=pl.CostEstimate(flops=20_000_000_000, bytes_accessed=40_000_000, transcendentals=0),
        name="other",
    )(table, grads, *pieces, *left, part)


def exchange(x, axis, d):
    if axis == "dp":
        pairs = [(v, SWAPS[d % 3](v)) for v in range(8)]
    else:
        pairs = [(f, 2 * SWAPS[d](f >> 1) + (f & 1)) for f in range(16)]
    return lax.ppermute(x, axis, pairs)


def apart(v, w):
    bits = [f(v) ^ f(w) for f in BITS]
    return next(u for u in range(8) if [f(u) for f in BITS] == bits)


def together(arrays):
    return list(lax.optimization_barrier(tuple(arrays)))


def precondition(sizes, table, grads, basis_in, eig_in, basis, eig_out):
    both = ("dp", "fsdp")
    every = [(d, q, c) for d in range(8) for q in range(8) for c in range(2)]
    inner = gather_own(table, basis_in, eig_in, sizes[0])
    inner = lax.ppermute(inner, both, [(d * 16 + q * 2 + c, d * 16 + 2 * apart(d, q) + c) for d, q, c in every])
    inner = lax.ppermute(inner, both, [(d * 16 + q * 2 + c, apart(d, q) * 16 + q * 2 + c) for d, q, c in every])

    shape, in_shape = (PIECE, WIDE), (IN_ROWS, 128)
    send, keep = pack(table, basis, eig_out, sizes[0])
    first = [exchange(send[t], "dp", t) for t in range(3)]
    second = [exchange(keep[t], "dp", t + 1) for t in range(3)]
    first = together(first)
    follow = [exchange(first[t], "dp", t + 1) for t in range(3)]
    in_first = exchange(inner, "fsdp", 0)
    in_second = exchange(inner, "fsdp", 1)
    arrived = together([*second, *follow])
    held = [[keep[t], first[t], arrived[t], arrived[3 + t]] for t in range(3)]
    send = route(table, (0, 1, 2), sizes[1], held, shape)
    third = [exchange(send[t], "dp", t + 2) for t in range(3)]
    in_first = together([in_first, *send])[0]
    in_follow = exchange(in_first, "fsdp", 1)
    in_held = [inner, in_first, in_second, in_follow]
    in_third = exchange(route(table, (3,), sizes[1], [in_held], in_shape)[0], "fsdp", 2)
    third = together(third)
    send = route(table, (0, 1, 2), M, [[*held[t], third[t]] for t in range(3)], shape)
    rest = [exchange(send[t], "dp", t) for t in range(3)]
    in_third = together([in_third, *send])[0]
    left = list(route(table, (3,), M, [[*in_held, in_third]], in_shape, PARTS))
    left += [lax.ppermute(x, "fsdp", [(f, f ^ 1) for f in range(16)]) for x in left]
    return chain_mine(table, grads, send, left), rest, left


def shards(grads, basis_in, eig_in, basis_out, eig_out, owner):
    table, tier = make_tables(jnp.swapaxes(owner, 0, 1))
    arrays = (
        table,
        jnp.swapaxes(grads.reshape(M, 640, 864), 1, 2),
        basis_in.reshape(M, 320, 128),
        eig_in,
        jnp.swapaxes(basis_out.reshape(M, 864, BO), 1, 2),
        eig_out,
    )
    plans = [functools.partial(precondition, sizes) for sizes in SIZES]
    part, rest, left = lax.switch(tier.reshape(()), plans, *arrays)
    result = chain_other(table, arrays[1], rest, left, part)
    return jnp.swapaxes(result, 1, 2).reshape(grads.shape)


def solution(mesh):
    placed = (
        P(None, None, "dp", "fsdp"),
        P(None, None, "dp", "fsdp", None),
        P(None, None, "dp", "fsdp"),
        P(None, None, "dp", "fsdp", None),
        P(None, None, "dp", "fsdp"),
        P(),
    )
    return jax.shard_map(
        shards, mesh=mesh, in_specs=placed, out_specs=P(None, None, "dp", "fsdp"), check_vma=False
    )
```

profile of v0, /device:TPU:0, one launch (start us, length us, event | category | flops | bytes accessed | tf_op | source)
XLA Modules:
  0.0 139.1 jit_solution(18367647172795476438)
XLA Ops:
  0.0 2.4 %tables.1 = (s32[115]{0:T(128)S(1)}, s32[1]{0:T(128)}) custom-call(s32[2,3]{1,0:T(2,128)} %bitcast.22), custom_call_target="tpu_custom_call" | custom-call | tf_op jit(solution)/shard_map/tables/pallas_call | solution.py:104
  3.1 115.6 %conditional.1 = (f32[6,864,640]{2,1,0:T(8,128)}, f32[6,48,896]{2,1,0:T(8,128)}, f32[6,48,896]{2,1,0:T(8,128)}, f32[6,48,896]{2,1,0:T(8,128)}, f32[2,336,128]{2,...) conditional(s32[]{:T(128)} %bitcast.3, (s32[115]{0:T(128)S(1)}, ...), branch_computations={%region_0.0_spmd, %region_1.0_spmd, %region_2.0_spmd} | conditional | flops 1000000 | bytes 165379440 | solution.py:409
  3.1 2.5 %gather.3 = f32[2,336,128]{2,1,0:T(8,128)} custom-call(s32[115]{0:T(128)S(1)} %get-tuple-element.41.table_ref, f32[6,320,128]{2,1,0:T(8,128)} %get-tuple-element.69.basis_ref, f32[3,2,1,320]{3,2,1,0:T(1,128)} %get-tuple-element.70.eig_ref), custom_call_target="tpu_custom_call" | custom-call | bytes 800000 | tf_op jit(solution)/shard_map/cond/branch_0_fun/gather/pallas_call | solution.py:176
  5.6 1.6 %collective-permute-start.12 = (f32[2,336,128]{2,1,0:T(8,128)}, f32[2,336,128]{2,1,0:T(8,128)S(1)}, u32[]{:S(2)}, u32[]{:S(2)}) collective-permute-start(f32[2,336,128]{2,1,0:T(8,128)} %gather.3), channel_id=1, source_target_pairs={{0,0},{1,1},{2,2},{3,3},{4,4},{5,5},{6,6},{7,7},{8,8},{9,9},{10,10... | collective-permute-start | bytes 1032200 | tf_op jit(solution)/shard_map/cond/branch_0_fun/ppermute | solution.py:370
  7.2 3.6 %pack.3 = (f32[2,48,896]{2,1,0:T(8,128)}, f32[2,48,896]{2,1,0:T(8,128)}, f32[2,48,896]{2,1,0:T(8,128)}, f32[2,48,896]{2,1,0:T(8,128)}, f32[2,48,896]{2,1,0:T(8,128)}, /*index=5*/f32[2,48,896]{2,1,0:T(8,128)}) custom-call(s32[115]{0:T(128)S(1)} %get-tuple-element.41.table_ref, ...), custom_call_target="tpu_custom_call" | custom-call | bytes 4000000 | tf_op jit(solution)/shard_map/cond/branch_0_fun/pack/pallas_call | solution.py:137
  10.8 4.1 %collective-permute-start = (f32[2,48,896]{2,1,0:T(8,128)}, f32[2,48,896]{2,1,0:T(8,128)S(1)}, u32[]{:S(2)}, u32[]{:S(2)}) collective-permute-start(f32[2,48,896]{2,1,0:T(8,128)} %get-tuple-element.46), channel_id=1, source_target_pairs={{0,64},{16,80},{32,96},{48,112},{64,0},{80,16},{96,32},{112,48},{1... | collective-permute-start | bytes 1032200 | tf_op jit(solution)/shard_map/cond/branch_0_fun/ppermute | solution.py:354
  14.9 2.9 %collective-permute-start.1 = (f32[2,48,896]{2,1,0:T(8,128)}, f32[2,48,896]{2,1,0:T(8,128)S(1)}, u32[]{:S(2)}, u32[]{:S(2)}) collective-permute-start(f32[2,48,896]{2,1,0:T(8,128)} %get-tuple-element.47), channel_id=1, source_target_pairs={{0,16},{16,0},{32,48},{48,32},{64,80},{80,64},{96,112},{112,96},{1... | collective-permute-start | bytes 1032200 | tf_op jit(solution)/shard_map/cond/branch_0_fun/ppermute | solution.py:354
  17.8 4.1 %collective-permute-start.2 = (f32[2,48,896]{2,1,0:T(8,128)}, f32[2,48,896]{2,1,0:T(8,128)S(1)}, u32[]{:S(2)}, u32[]{:S(2)}) collective-permute-start(f32[2,48,896]{2,1,0:T(8,128)} %get-tuple-element.48), channel_id=1, source_target_pairs={{0,48},{16,32},{32,16},{48,0},{64,112},{80,96},{96,80},{112,64},{1... | collective-permute-start | bytes 1032200 | tf_op jit(solution)/shard_map/cond/branch_0_fun/ppermute | solution.py:354
  23.4 3.1 %collective-permute-done.refs_1_ = f32[2,48,896]{2,1,0:T(8,128)S(1)} collective-permute-done((f32[2,48,896]{2,1,0:T(8,128)}, f32[2,48,896]{2,1,0:T(8,128)S(1)}, u32[]{:S(2)}, u32[]{:S(2)}) %collective-permute-start) | collective-permute-done | bytes 344096 | tf_op jit(solution)/shard_map/cond/branch_0_fun/ppermute | solution.py:354
  27.6 3.6 %collective-permute-done.2.refs_9_.refs_11_ = f32[2,48,896]{2,1,0:T(8,128)S(1)} collective-permute-done((f32[2,48,896]{2,1,0:T(8,128)}, f32[2,48,896]{2,1,0:T(8,128)S(1)}, u32[]{:S(2)}, u32[]{:S(2)}) %collective-permute-start.2) | collective-permute-done | bytes 344096 | tf_op jit(solution)/shard_map/cond/branch_0_fun/ppermute | solution.py:354
  32.0 2.4 %collective-permute-done.3.refs_2_ = f32[2,48,896]{2,1,0:T(8,128)S(1)} collective-permute-done((f32[2,48,896]{2,1,0:T(8,128)}, f32[2,48,896]{2,1,0:T(8,128)S(1)}, u32[]{:S(2)}, u32[]{:S(2)}) %collective-permute-start.3) | collective-permute-done | bytes 344096 | tf_op jit(solution)/shard_map/cond/branch_0_fun/ppermute | solution.py:354
  34.4 5.6 %collective-permute-start.7 = (f32[2,48,896]{2,1,0:T(8,128)S(1)}, f32[2,48,896]{2,1,0:T(8,128)S(1)}, u32[]{:S(2)}, u32[]{:S(2)}) collective-permute-start(f32[2,48,896]{2,1,0:T(8,128)S(1)} %collective-permute-done.1.refs_5_.refs_6_), channel_id=1, source_target_pairs={{0,48},{16,32},{32,16},{48,0},{64,112},{80,96},{96,80},{112,64},{1... | collective-permute-start | bytes 1032200 | tf_op jit(solution)/shard_map/cond/branch_0_fun/ppermute | solution.py:354
  40.1 1.3 collective-permute-start.14
  41.4 3.8 %collective-permute-done.7.refs_7_.refs_8_ = f32[2,48,896]{2,1,0:T(8,128)S(1)} collective-permute-done((f32[2,48,896]{2,1,0:T(8,128)S(1)}, f32[2,48,896]{2,1,0:T(8,128)S(1)}, u32[]{:S(2)}, u32[]{:S(2)}) %collective-permute-start.7) | collective-permute-done | bytes 344096 | tf_op jit(solution)/shard_map/cond/branch_0_fun/ppermute | solution.py:354
  45.2 4.8 %collective-permute-done.8.refs_11_.refs_13_ = f32[2,48,896]{2,1,0:T(8,128)} collective-permute-done((f32[2,48,896]{2,1,0:T(8,128)S(1)}, f32[2,48,896]{2,1,0:T(8,128)}, u32[]{:S(2)}, u32[]{:S(2)}) %collective-permute-start.8) | collective-permute-done | bytes 344096 | tf_op jit(solution)/shard_map/cond/branch_0_fun/ppermute | solution.py:354
  50.1 4.0 %route.12 = (f32[5,48,896]{2,1,0:T(8,128)}, f32[5,48,896]{2,1,0:T(8,128)}, f32[5,48,896]{2,1,0:T(8,128)}) custom-call(s32[115]{0:T(128)S(1)} %get-tuple-element.41.table_ref, f32[2,48,896]{2,1,0:T(8,128)} %get-tuple-element.45.refs_0_, f32[2,48,896]{2,1,0:T(8,128)} %copy-done.25, f32[2,48,896]{2,1,0:T(8,128)} %copy-done.28, f32[2,48,896]{2,1,0:T(8,128)} %copy-done.31, ...), custom_call_target="tpu_custom_call" | custom-call | bytes 2000000 | tf_op jit(solution)/shard_map/cond/branch_0_fun/route/pallas_call | solution.py:210
  55.0 4.7 %collective-permute-done.14.refs_1_ = f32[2,336,128]{2,1,0:T(8,128)S(1)} collective-permute-done((f32[2,336,128]{2,1,0:T(8,128)S(1)}, f32[2,336,128]{2,1,0:T(8,128)S(1)}, u32[]{:S(2)}, u32[]{:S(2)}) %collective-permute-start.14) | collective-permute-done | bytes 344096 | tf_op jit(solution)/shard_map/cond/branch_0_fun/ppermute | solution.py:354
  59.7 2.0 %collective-permute-start.16 = (f32[2,336,128]{2,1,0:T(8,128)S(1)}, f32[2,336,128]{2,1,0:T(8,128)S(1)}, u32[]{:S(2)}, u32[]{:S(2)}) collective-permute-start(f32[2,336,128]{2,1,0:T(8,128)S(1)} %collective-permute-done.14.refs_1_), channel_id=1, source_target_pairs={{0,2},{1,3},{2,0},{3,1},{4,6},{5,7},{6,4},{7,5},{8,10},{9,11},{10,... | collective-permute-start | bytes 1032200 | tf_op jit(solution)/shard_map/cond/branch_0_fun/ppermute | solution.py:354
  61.7 5.0 %collective-permute-start.9 = (f32[5,48,896]{2,1,0:T(8,128)}, f32[5,48,896]{2,1,0:T(8,128)S(1)}, u32[]{:S(2)}, u32[]{:S(2)}) collective-permute-start(f32[5,48,896]{2,1,0:T(8,128)} %get-tuple-element.60), channel_id=1, source_target_pairs={{0,48},{16,32},{32,16},{48,0},{64,112},{80,96},{96,80},{112,64},{1... | collective-permute-start | bytes 2580488 | tf_op jit(solution)/shard_map/cond/branch_0_fun/ppermute | solution.py:354
  66.7 2.1 %collective-permute-start.10 = (f32[5,48,896]{2,1,0:T(8,128)}, f32[5,48,896]{2,1,0:T(8,128)S(1)}, u32[]{:S(2)}, u32[]{:S(2)}) collective-permute-start(f32[5,48,896]{2,1,0:T(8,128)} %get-tuple-element.61), channel_id=1, source_target_pairs={{0,64},{16,80},{32,96},{48,112},{64,0},{80,16},{96,32},{112,48},{1... | collective-permute-start | bytes 2580488 | tf_op jit(solution)/shard_map/cond/branch_0_fun/ppermute | solution.py:354
  70.3 2.8 %route.14 = f32[5,336,128]{2,1,0:T(8,128)} custom-call(s32[115]{0:T(128)S(1)} %get-tuple-element.41.table_ref, f32[2,336,128]{2,1,0:T(8,128)} %copy-done.21, f32[2,336,128]{2,1,0:T(8,128)} %copy-done.22, f32[2,336,128]{2,1,0:T(8,128)} %copy-done.23, f32[2,336,128]{2,1,0:T(8,128)} %copy-done.24), custom_call_target="tpu_custom_call" | custom-call | bytes 2000000 | tf_op jit(solution)/shard_map/cond/branch_0_fun/route/pallas_call | solution.py:210
  73.0 3.9 %collective-permute-start.17 = (f32[5,336,128]{2,1,0:T(8,128)}, f32[5,336,128]{2,1,0:T(8,128)S(1)}, u32[]{:S(2)}, u32[]{:S(2)}) collective-permute-start(f32[5,336,128]{2,1,0:T(8,128)} %route.14), channel_id=1, source_target_pairs={{0,6},{1,7},{2,4},{3,5},{4,2},{5,3},{6,0},{7,1},{8,14},{9,15},{10,... | collective-permute-start | bytes 2580488 | tf_op jit(solution)/shard_map/cond/branch_0_fun/ppermute | solution.py:354
  76.9 7.1 %collective-permute-done.9.refs_4_ = f32[5,48,896]{2,1,0:T(8,128)S(1)} collective-permute-done((f32[5,48,896]{2,1,0:T(8,128)}, f32[5,48,896]{2,1,0:T(8,128)S(1)}, u32[]{:S(2)}, u32[]{:S(2)}) %collective-permute-start.9) | collective-permute-done | bytes 860192 | tf_op jit(solution)/shard_map/cond/branch_0_fun/ppermute | solution.py:354
  84.0 1.5 %collective-permute-done.10.refs_9_ = f32[5,48,896]{2,1,0:T(8,128)S(1)} collective-permute-done((f32[5,48,896]{2,1,0:T(8,128)}, f32[5,48,896]{2,1,0:T(8,128)S(1)}, u32[]{:S(2)}, u32[]{:S(2)}) %collective-permute-start.10) | collective-permute-done | bytes 860192 | tf_op jit(solution)/shard_map/cond/branch_0_fun/ppermute | solution.py:354
  85.5 1.5 %collective-permute-done.11.refs_14_ = f32[5,48,896]{2,1,0:T(8,128)} collective-permute-done((f32[5,48,896]{2,1,0:T(8,128)}, f32[5,48,896]{2,1,0:T(8,128)}, u32[]{:S(2)}, u32[]{:S(2)}) %collective-permute-start.11) | collective-permute-done | bytes 860192 | tf_op jit(solution)/shard_map/cond/branch_0_fun/ppermute | solution.py:354
  87.0 4.3 %route.13 = (f32[6,48,896]{2,1,0:T(8,128)}, f32[6,48,896]{2,1,0:T(8,128)}, f32[6,48,896]{2,1,0:T(8,128)}) custom-call(s32[115]{0:T(128)S(1)} %get-tuple-element.41.table_ref, f32[2,48,896]{2,1,0:T(8,128)} %get-tuple-element.45.refs_0_, f32[2,48,896]{2,1,0:T(8,128)} %copy-done.25, f32[2,48,896]{2,1,0:T(8,128)} %copy-done.28, f32[2,48,896]{2,1,0:T(8,128)} %copy-done.31, ...), custom_call_target="tpu_custom_call" | custom-call | bytes 2400000 | tf_op jit(solution)/shard_map/cond/branch_0_fun/route/pallas_call | solution.py:210
  92.6 1.7 %collective-permute-start.23 = (f32[6,48,896]{2,1,0:T(8,128)}, f32[6,48,896]{2,1,0:T(8,128)}, u32[]{:S(2)}, u32[]{:S(2)}) collective-permute-start(f32[6,48,896]{2,1,0:T(8,128)} %get-tuple-element.68.p2), channel_id=1, source_target_pairs={{0,48},{16,32},{32,16},{48,0},{64,112},{80,96},{96,80},{112,64},{1... | collective-permute-start | bytes 3096584 | tf_op jit(solution)/shard_map/cond/branch_0_fun/ppermute | solution.py:354
  95.2 2.9 %route.15 = (f32[2,336,128]{2,1,0:T(8,128)}, f32[2,336,128]{2,1,0:T(8,128)}, f32[2,336,128]{2,1,0:T(8,128)}) custom-call(s32[115]{0:T(128)S(1)} %get-tuple-element.41.table_ref, f32[2,336,128]{2,1,0:T(8,128)} %copy-done.21, f32[2,336,128]{2,1,0:T(8,128)} %copy-done.22, f32[2,336,128]{2,1,0:T(8,128)} %copy-done.23, f32[2,336,128]{2,1,0:T(8,128)} %copy-done.24, ...), custom_call_target="tpu_custom_call" | custom-call | bytes 2400000 | tf_op jit(solution)/shard_map/cond/branch_0_fun/route/pallas_call | solution.py:210
  98.7 1.5 %collective-permute-done.18.refs_3_ = f32[2,336,128]{2,1,0:T(8,128)} collective-permute-done((f32[2,336,128]{2,1,0:T(8,128)}, f32[2,336,128]{2,1,0:T(8,128)}, u32[]{:S(2)}, u32[]{:S(2)}) %collective-permute-start.18) | collective-permute-done | bytes 344096 | tf_op jit(solution)/shard_map/cond/branch_0_fun/ppermute | solution.py:394
  100.7 1.5 %collective-permute-done.20.refs_5_ = f32[2,336,128]{2,1,0:T(8,128)} collective-permute-done((f32[2,336,128]{2,1,0:T(8,128)}, f32[2,336,128]{2,1,0:T(8,128)}, u32[]{:S(2)}, u32[]{:S(2)}) %collective-permute-start.20) | collective-permute-done | bytes 344096 | tf_op jit(solution)/shard_map/cond/branch_0_fun/ppermute | solution.py:394
  102.2 16.2 %mine.3 = f32[6,864,640]{2,1,0:T(8,128)} custom-call(s32[115]{0:T(128)S(1)} %get-tuple-element.41.table_ref, bf16[6,864,640]{2,1,0:T(8,128)(2,1)} %get-tuple-element.42.grad_ref, f32[6,48,896]{2,1,0:T(8,128)} %get-tuple-element.66.p0, f32[6,48,896]{2,1,0:T(8,128)} %get-tuple-element.67.p1, f32[6,48,896]{2,1,0:T(8,128)} %get-tuple-element.68.p2, ...), custom_call_target="tpu_custom_call" | custom-call | flops 1000000 | bytes 1000000 | tf_op jit(solution)/shard_map/cond/branch_0_fun/mine/pallas_call | solution.py:316
  118.7 20.4 %other.1 = bf16[6,864,640]{2,1,0:T(8,128)(2,1)} custom-call(s32[115]{0:T(128)S(1)} %get-tuple-element.158.table_ref, bf16[6,864,640]{2,1,0:T(8,128)(2,1)} %bitcast.18, f32[6,48,896]{2,1,0:T(8,128)} %get-tuple-element.160.p0, f32[6,48,896]{2,1,0:T(8,128)} %get-tuple-element.161.p1, f32[6,48,896]{2,1,0:T(8,128)} %get-tuple-element.162.p2, ...), custom_call_target="tpu_custom_call" | custom-call | flops 20000000000 | bytes 40000000 | tf_op jit(solution)/shard_map/other/pallas_call | solution.py:333
  (56 shorter events, 9.1 us)
Async XLA Ops:
  5.6 17.2 %collective-permute-start.12 = (f32[2,336,128]{2,1,0:T(8,128)}, f32[2,336,128]{2,1,0:T(8,128)S(1)}, u32[]{:S(2)}, u32[]{:S(2)}) collective-permute-start(f32[2,336,128]{2,1,0:T(8,128)} %gather.3), channel_id=1, source_target_pairs={{0,0},{1,1},{2,2},{3,3},{4,4},{5,5},{6,6},{7,7},{8,8},{9,9},{10,10... | collective-permute-start | bytes 1032200 | tf_op jit(solution)/shard_map/cond/branch_0_fun/ppermute | solution.py:370
  10.8 15.7 %collective-permute-start = (f32[2,48,896]{2,1,0:T(8,128)}, f32[2,48,896]{2,1,0:T(8,128)S(1)}, u32[]{:S(2)}, u32[]{:S(2)}) collective-permute-start(f32[2,48,896]{2,1,0:T(8,128)} %get-tuple-element.46), channel_id=1, source_target_pairs={{0,64},{16,80},{32,96},{48,112},{64,0},{80,16},{96,32},{112,48},{1... | collective-permute-start | bytes 1032200 | tf_op jit(solution)/shard_map/cond/branch_0_fun/ppermute | solution.py:354
  14.9 12.3 %collective-permute-start.1 = (f32[2,48,896]{2,1,0:T(8,128)}, f32[2,48,896]{2,1,0:T(8,128)S(1)}, u32[]{:S(2)}, u32[]{:S(2)}) collective-permute-start(f32[2,48,896]{2,1,0:T(8,128)} %get-tuple-element.47), channel_id=1, source_target_pairs={{0,16},{16,0},{32,48},{48,32},{64,80},{80,64},{96,112},{112,96},{1... | collective-permute-start | bytes 1032200 | tf_op jit(solution)/shard_map/cond/branch_0_fun/ppermute | solution.py:354
  17.8 13.3 %collective-permute-start.2 = (f32[2,48,896]{2,1,0:T(8,128)}, f32[2,48,896]{2,1,0:T(8,128)S(1)}, u32[]{:S(2)}, u32[]{:S(2)}) collective-permute-start(f32[2,48,896]{2,1,0:T(8,128)} %get-tuple-element.48), channel_id=1, source_target_pairs={{0,48},{16,32},{32,16},{48,0},{64,112},{80,96},{96,80},{112,64},{1... | collective-permute-start | bytes 1032200 | tf_op jit(solution)/shard_map/cond/branch_0_fun/ppermute | solution.py:354
  22.0 12.4 %collective-permute-start.3 = (f32[2,48,896]{2,1,0:T(8,128)}, f32[2,48,896]{2,1,0:T(8,128)S(1)}, u32[]{:S(2)}, u32[]{:S(2)}) collective-permute-start(f32[2,48,896]{2,1,0:T(8,128)} %get-tuple-element.45.refs_0_), channel_id=1, source_target_pairs={{0,16},{16,0},{32,48},{48,32},{64,80},{80,64},{96,112},{112,96},{1... | collective-permute-start | bytes 1032200 | tf_op jit(solution)/shard_map/cond/branch_0_fun/ppermute | solution.py:354
  22.8 17.2 %collective-permute-start.4 = (f32[2,48,896]{2,1,0:T(8,128)}, f32[2,48,896]{2,1,0:T(8,128)S(1)}, u32[]{:S(2)}, u32[]{:S(2)}) collective-permute-start(f32[2,48,896]{2,1,0:T(8,128)} %get-tuple-element.50.refs_4_.refs_5_), channel_id=1, source_target_pairs={{0,48},{16,32},{32,16},{48,0},{64,112},{80,96},{96,80},{112,64},{1... | collective-permute-start | bytes 1032200 | tf_op jit(solution)/shard_map/cond/branch_0_fun/ppermute | solution.py:354
  26.5 23.5 %copy-start.25 = (f32[2,48,896]{2,1,0:T(8,128)}, f32[2,48,896]{2,1,0:T(8,128)S(1)}, u32[]{:S(2)}) copy-start(f32[2,48,896]{2,1,0:T(8,128)S(1)} %collective-permute-done.refs_1_) | copy-start | bytes 1032196 | tf_op jit(solution)/shard_map/cond
  26.5 13.5 %collective-permute-start.13 = (f32[2,336,128]{2,1,0:T(8,128)S(1)}, f32[2,336,128]{2,1,0:T(8,128)S(1)}, u32[]{:S(2)}, u32[]{:S(2)}) collective-permute-start(f32[2,336,128]{2,1,0:T(8,128)S(1)} %collective-permute-done.12), channel_id=1, source_target_pairs={{0,0},{1,1},{2,18},{3,19},{4,36},{5,37},{6,54},{7,55},{8,72},{9,73... | collective-permute-start | bytes 1032200 | tf_op jit(solution)/shard_map/cond/branch_0_fun/ppermute | solution.py:371
  27.2 22.8 %copy-start.26 = (f32[2,48,896]{2,1,0:T(8,128)}, f32[2,48,896]{2,1,0:T(8,128)S(1)}, u32[]{:S(2)}) copy-start(f32[2,48,896]{2,1,0:T(8,128)S(1)} %collective-permute-done.1.refs_5_.refs_6_) | copy-start | bytes 1032196 | tf_op jit(solution)/shard_map/cond
  27.2 14.2 %collective-permute-start.5 = (f32[2,48,896]{2,1,0:T(8,128)}, f32[2,48,896]{2,1,0:T(8,128)S(1)}, u32[]{:S(2)}, u32[]{:S(2)}) collective-permute-start(f32[2,48,896]{2,1,0:T(8,128)} %get-tuple-element.51.refs_8_.refs_10_), channel_id=1, source_target_pairs={{0,64},{16,80},{32,96},{48,112},{64,0},{80,16},{96,32},{112,48},{1... | collective-permute-start | bytes 1032200 | tf_op jit(solution)/shard_map/cond/branch_0_fun/ppermute | solution.py:354
  31.2 18.9 %copy-start.27 = (f32[2,48,896]{2,1,0:T(8,128)}, f32[2,48,896]{2,1,0:T(8,128)S(1)}, u32[]{:S(2)}) copy-start(f32[2,48,896]{2,1,0:T(8,128)S(1)} %collective-permute-done.2.refs_9_.refs_11_) | copy-start | bytes 1032196 | tf_op jit(solution)/shard_map/cond
  31.2 10.3 %collective-permute-start.6 = (f32[2,48,896]{2,1,0:T(8,128)S(1)}, f32[2,48,896]{2,1,0:T(8,128)S(1)}, u32[]{:S(2)}, u32[]{:S(2)}) collective-permute-start(f32[2,48,896]{2,1,0:T(8,128)S(1)} %collective-permute-done.refs_1_), channel_id=1, source_target_pairs={{0,16},{16,0},{32,48},{48,32},{64,80},{80,64},{96,112},{112,96},{1... | collective-permute-start | bytes 1032200 | tf_op jit(solution)/shard_map/cond/branch_0_fun/ppermute | solution.py:354
  34.4 15.7 %copy-start.28 = (f32[2,48,896]{2,1,0:T(8,128)}, f32[2,48,896]{2,1,0:T(8,128)S(1)}, u32[]{:S(2)}) copy-start(f32[2,48,896]{2,1,0:T(8,128)S(1)} %collective-permute-done.3.refs_2_) | copy-start | bytes 1032196 | tf_op jit(solution)/shard_map/cond
  34.4 10.8 %collective-permute-start.7 = (f32[2,48,896]{2,1,0:T(8,128)S(1)}, f32[2,48,896]{2,1,0:T(8,128)S(1)}, u32[]{:S(2)}, u32[]{:S(2)}) collective-permute-start(f32[2,48,896]{2,1,0:T(8,128)S(1)} %collective-permute-done.1.refs_5_.refs_6_), channel_id=1, source_target_pairs={{0,48},{16,32},{32,16},{48,0},{64,112},{80,96},{96,80},{112,64},{1... | collective-permute-start | bytes 1032200 | tf_op jit(solution)/shard_map/cond/branch_0_fun/ppermute | solution.py:354
  40.0 10.1 %copy-start.29 = (f32[2,48,896]{2,1,0:T(8,128)}, f32[2,48,896]{2,1,0:T(8,128)S(1)}, u32[]{:S(2)}) copy-start(f32[2,48,896]{2,1,0:T(8,128)S(1)} %collective-permute-done.4.refs_6_.refs_7_) | copy-start | bytes 1032196 | tf_op jit(solution)/shard_map/cond
  40.0 10.1 %collective-permute-start.8 = (f32[2,48,896]{2,1,0:T(8,128)S(1)}, f32[2,48,896]{2,1,0:T(8,128)}, u32[]{:S(2)}, u32[]{:S(2)}) collective-permute-start(f32[2,48,896]{2,1,0:T(8,128)S(1)} %collective-permute-done.2.refs_9_.refs_11_), channel_id=1, source_target_pairs={{0,64},{16,80},{32,96},{48,112},{64,0},{80,16},{96,32},{112,48},{1... | collective-permute-start | bytes 1032200 | tf_op jit(solution)/shard_map/cond/branch_0_fun/ppermute | solution.py:354
  40.1 28.7 %copy-start.21 = (f32[2,336,128]{2,1,0:T(8,128)}, f32[2,336,128]{2,1,0:T(8,128)S(1)}, u32[]{:S(2)}) copy-start(f32[2,336,128]{2,1,0:T(8,128)S(1)} %collective-permute-done.13.refs_0_) | copy-start | bytes 1032196 | tf_op jit(solution)/shard_map/cond
  40.1 19.7 %collective-permute-start.14 = (f32[2,336,128]{2,1,0:T(8,128)S(1)}, f32[2,336,128]{2,1,0:T(8,128)S(1)}, u32[]{:S(2)}, u32[]{:S(2)}) collective-permute-start(f32[2,336,128]{2,1,0:T(8,128)S(1)} %collective-permute-done.13.refs_0_), channel_id=1, source_target_pairs={{0,8},{1,9},{2,10},{3,11},{4,12},{5,13},{6,14},{7,15},{8,0},{9,1},... | collective-permute-start | bytes 1032200 | tf_op jit(solution)/shard_map/cond/branch_0_fun/ppermute | solution.py:354
  41.4 8.7 %copy-start.31 = (f32[2,48,896]{2,1,0:T(8,128)}, f32[2,48,896]{2,1,0:T(8,128)S(1)}, u32[]{:S(2)}) copy-start(f32[2,48,896]{2,1,0:T(8,128)S(1)} %collective-permute-done.6.refs_3_) | copy-start | bytes 1032196 | tf_op jit(solution)/shard_map/cond
  54.1 14.7 %collective-permute-start.15 = (f32[2,336,128]{2,1,0:T(8,128)S(1)}, f32[2,336,128]{2,1,0:T(8,128)S(1)}, u32[]{:S(2)}, u32[]{:S(2)}) collective-permute-start(f32[2,336,128]{2,1,0:T(8,128)S(1)} %collective-permute-done.13.refs_0_), channel_id=1, source_target_pairs={{0,2},{1,3},{2,0},{3,1},{4,6},{5,7},{6,4},{7,5},{8,10},{9,11},{10,... | collective-permute-start | bytes 1032200 | tf_op jit(solution)/shard_map/cond/branch_0_fun/ppermute | solution.py:354
  59.7 9.1 %copy-start.22 = (f32[2,336,128]{2,1,0:T(8,128)}, f32[2,336,128]{2,1,0:T(8,128)S(1)}, u32[]{:S(2)}) copy-start(f32[2,336,128]{2,1,0:T(8,128)S(1)} %collective-permute-done.14.refs_1_) | copy-start | bytes 1032196 | tf_op jit(solution)/shard_map/cond
  59.7 9.1 %collective-permute-start.16 = (f32[2,336,128]{2,1,0:T(8,128)S(1)}, f32[2,336,128]{2,1,0:T(8,128)S(1)}, u32[]{:S(2)}, u32[]{:S(2)}) collective-permute-start(f32[2,336,128]{2,1,0:T(8,128)S(1)} %collective-permute-done.14.refs_1_), channel_id=1, source_target_pairs={{0,2},{1,3},{2,0},{3,1},{4,6},{5,7},{6,4},{7,5},{8,10},{9,11},{10,... | collective-permute-start | bytes 1032200 | tf_op jit(solution)/shard_map/cond/branch_0_fun/ppermute | solution.py:354
  61.7 22.3 %collective-permute-start.9 = (f32[5,48,896]{2,1,0:T(8,128)}, f32[5,48,896]{2,1,0:T(8,128)S(1)}, u32[]{:S(2)}, u32[]{:S(2)}) collective-permute-start(f32[5,48,896]{2,1,0:T(8,128)} %get-tuple-element.60), channel_id=1, source_target_pairs={{0,48},{16,32},{32,16},{48,0},{64,112},{80,96},{96,80},{112,64},{1... | collective-permute-start | bytes 2580488 | tf_op jit(solution)/shard_map/cond/branch_0_fun/ppermute | solution.py:354
  66.7 18.8 %collective-permute-start.10 = (f32[5,48,896]{2,1,0:T(8,128)}, f32[5,48,896]{2,1,0:T(8,128)S(1)}, u32[]{:S(2)}, u32[]{:S(2)}) collective-permute-start(f32[5,48,896]{2,1,0:T(8,128)} %get-tuple-element.61), channel_id=1, source_target_pairs={{0,64},{16,80},{32,96},{48,112},{64,0},{80,16},{96,32},{112,48},{1... | collective-permute-start | bytes 2580488 | tf_op jit(solution)/shard_map/cond/branch_0_fun/ppermute | solution.py:354
  68.8 18.3 %collective-permute-start.11 = (f32[5,48,896]{2,1,0:T(8,128)}, f32[5,48,896]{2,1,0:T(8,128)}, u32[]{:S(2)}, u32[]{:S(2)}) collective-permute-start(f32[5,48,896]{2,1,0:T(8,128)} %get-tuple-element.62), channel_id=1, source_target_pairs={{0,16},{16,0},{32,48},{48,32},{64,80},{80,64},{96,112},{112,96},{1... | collective-permute-start | bytes 2580488 | tf_op jit(solution)/shard_map/cond/branch_0_fun/ppermute | solution.py:354
  73.0 21.3 %collective-permute-start.17 = (f32[5,336,128]{2,1,0:T(8,128)}, f32[5,336,128]{2,1,0:T(8,128)S(1)}, u32[]{:S(2)}, u32[]{:S(2)}) collective-permute-start(f32[5,336,128]{2,1,0:T(8,128)} %route.14), channel_id=1, source_target_pairs={{0,6},{1,7},{2,4},{3,5},{4,2},{5,3},{6,0},{7,1},{8,14},{9,15},{10,... | collective-permute-start | bytes 2580488 | tf_op jit(solution)/shard_map/cond/branch_0_fun/ppermute | solution.py:354
  91.4 27.1 %collective-permute-start.21 = (f32[6,48,896]{2,1,0:T(8,128)}, f32[6,48,896]{2,1,0:T(8,128)}, u32[]{:S(2)}, u32[]{:S(2)}) collective-permute-start(f32[6,48,896]{2,1,0:T(8,128)} %get-tuple-element.66.p0), channel_id=1, source_target_pairs={{0,64},{16,80},{32,96},{48,112},{64,0},{80,16},{96,32},{112,48},{1... | collective-permute-start | bytes 3096584 | tf_op jit(solution)/shard_map/cond/branch_0_fun/ppermute | solution.py:354
  92.5 25.9 %collective-permute-start.22 = (f32[6,48,896]{2,1,0:T(8,128)}, f32[6,48,896]{2,1,0:T(8,128)}, u32[]{:S(2)}, u32[]{:S(2)}) collective-permute-start(f32[6,48,896]{2,1,0:T(8,128)} %get-tuple-element.67.p1), channel_id=1, source_target_pairs={{0,16},{16,0},{32,48},{48,32},{64,80},{80,64},{96,112},{112,96},{1... | collective-permute-start | bytes 3096584 | tf_op jit(solution)/shard_map/cond/branch_0_fun/ppermute | solution.py:354
  92.6 25.9 %collective-permute-start.23 = (f32[6,48,896]{2,1,0:T(8,128)}, f32[6,48,896]{2,1,0:T(8,128)}, u32[]{:S(2)}, u32[]{:S(2)}) collective-permute-start(f32[6,48,896]{2,1,0:T(8,128)} %get-tuple-element.68.p2), channel_id=1, source_target_pairs={{0,48},{16,32},{32,16},{48,0},{64,112},{80,96},{96,80},{112,64},{1... | collective-permute-start | bytes 3096584 | tf_op jit(solution)/shard_map/cond/branch_0_fun/ppermute | solution.py:354
  98.1 2.1 %collective-permute-start.18 = (f32[2,336,128]{2,1,0:T(8,128)}, f32[2,336,128]{2,1,0:T(8,128)}, u32[]{:S(2)}, u32[]{:S(2)}) collective-permute-start(f32[2,336,128]{2,1,0:T(8,128)} %get-tuple-element.174.refs_0_), channel_id=1, source_target_pairs={{0,1},{1,0},{2,3},{3,2},{4,5},{5,4},{6,7},{7,6},{8,9},{9,8},{10,11... | collective-permute-start | bytes 1032200 | tf_op jit(solution)/shard_map/cond/branch_0_fun/ppermute | solution.py:394
  98.2 2.5 %collective-permute-start.19 = (f32[2,336,128]{2,1,0:T(8,128)}, f32[2,336,128]{2,1,0:T(8,128)}, u32[]{:S(2)}, u32[]{:S(2)}) collective-permute-start(f32[2,336,128]{2,1,0:T(8,128)} %get-tuple-element.175.refs_1_), channel_id=1, source_target_pairs={{0,1},{1,0},{2,3},{3,2},{4,5},{5,4},{6,7},{7,6},{8,9},{9,8},{10,11... | collective-permute-start | bytes 1032200 | tf_op jit(solution)/shard_map/cond/branch_0_fun/ppermute | solution.py:394
  100.2 2.0 %collective-permute-start.20 = (f32[2,336,128]{2,1,0:T(8,128)}, f32[2,336,128]{2,1,0:T(8,128)}, u32[]{:S(2)}, u32[]{:S(2)}) collective-permute-start(f32[2,336,128]{2,1,0:T(8,128)} %get-tuple-element.176.refs_2_), channel_id=1, source_target_pairs={{0,1},{1,0},{2,3},{3,2},{4,5},{5,4},{6,7},{7,6},{8,9},{9,8},{10,11... | collective-permute-start | bytes 1032200 | tf_op jit(solution)/shard_map/cond/branch_0_fun/ppermute | solution.py:394
  (7 other events, 20.5 us)
where the time goes:
time: 141 us; the launch traced here: 139 us
  Pallas kernels  59 us (42%)
  starting transfers between devices  40.6 us (29%)
  waiting for transfers between devices  35.9 us (25%)
  local copies, waits for them, and re-layouts  2.42 us (2%)
    ppermute x19, starting transfers between devices, exchange(): return lax.ppermute(x, axis, pairs)  37.6 us
    ppermute x19, waiting for transfers between devices, exchange(): return lax.ppermute(x, axis, pairs)  32.6 us
    pallas_call x1, Pallas kernels, chain_other(): pl.pallas_call(other_kernel, out_shape=jax.ShapeDtypeStruct((M, 864, 640)...  20.4 us
    pallas_call x1, Pallas kernels, chain_mine(): pl.pallas_call(mine_kernel, out_shape=jax.ShapeDtypeStruct((M, 864, 640),...  16.2 us
    pallas_call x4, Pallas kernels, route(): pl.pallas_call(functools.partial(route_kernel, chains, slots, count, part...  14 us
    pallas_call x1, Pallas kernels, pack(): pl.pallas_call(pack_kernel, out_shape=[jax.ShapeDtypeStruct((slots, PIECE...  3.63 us
    ppermute x3, waiting for transfers between devices, precondition(): lax.ppermute(x, 'fsdp', [(f, f ^ 1) for f in range(16)])  3.34 us
  transfers between devices with their start and end apart: 24, of which 12 were waited for; matrix products, arithmetic and copies ran while one was open for 0% of the time, Pallas kernels for 24%

commit v1 on v0

--- a/solution.py
+++ b/solution.py
@@ -42,7 +42,7 @@
     return pl.BlockSpec((1, *shape), lambda m, *_: (m,) + (0,) * len(shape))
 
 
-CHAINS = ((0, 0), (1, 0), (2, 0), (0, 1))
+CHAINS = ((0, 1, 2, 0), (1, 2, 0, 0), (2, 0, 1, 0), (0, 2, 1, 1))
 LIST = 7
 THIRD = 2 * M
 CHAIN = THIRD + 2 * LIST
@@ -54,23 +54,21 @@
 
 
 def table_kernel(owner_ref, out_ref, tier_ref):
-    def clear(i, carry):
-        out_ref[i] = 0
-        return carry
-
-    lax.fori_loop(0, TABLE, clear, 0)
+    for start, length in [(c * CHAIN + THIRD, 2 * LIST) for c in range(len(CHAINS))] + [(OWN, LIST)]:
+        for i in range(length):
+            out_ref[start + i] = 0
     owners = [owner_ref[m % 2, m // 2] for m in range(M)]
     corner = [[BITS[d](v) for v in owners] for d in range(3)]
     at, over = lax.axis_index("dp"), lax.axis_index("fsdp")
     row = [BITS[d](at) for d in range(3)]
     column = [BITS[d](over >> 1) for d in range(3)]
-    for c, (turn, axis) in enumerate(CHAINS):
+    for c, (*order, axis) in enumerate(CHAINS):
         seen = [jnp.int32(0)] * 5
         spot = jnp.int32(0)
         for m in range(M):
-            away = [corner[(turn + e) % 3][m] ^ row[(turn + e) % 3] for e in range(3)]
+            away = [corner[d][m] ^ row[d] for d in order]
             if axis:
-                away = [away[e] ^ column[(turn + e) % 3] for e in range(3)]
+                away = [away[e] ^ column[order[e]] for e in range(3)]
             array = jnp.where(away[2] == 1, 4, away[0] + 2 * away[1])
             slot = seen[0]
             for k in range(1, 5):
@@ -377,15 +375,15 @@
     first = together(first)
     follow = [exchange(first[t], "dp", t + 1) for t in range(3)]
     in_first = exchange(inner, "fsdp", 0)
-    in_second = exchange(inner, "fsdp", 1)
+    in_second = exchange(inner, "fsdp", 2)
     arrived = together([*second, *follow])
     held = [[keep[t], first[t], arrived[t], arrived[3 + t]] for t in range(3)]
     send = route(table, (0, 1, 2), sizes[1], held, shape)
     third = [exchange(send[t], "dp", t + 2) for t in range(3)]
     in_first = together([in_first, *send])[0]
-    in_follow = exchange(in_first, "fsdp", 1)
+    in_follow = exchange(in_first, "fsdp", 2)
     in_held = [inner, in_first, in_second, in_follow]
-    in_third = exchange(route(table, (3,), sizes[1], [in_held], in_shape)[0], "fsdp", 2)
+    in_third = exchange(route(table, (3,), sizes[1], [in_held], in_shape)[0], "fsdp", 1)
     third = together(third)
     send = route(table, (0, 1, 2), M, [[*held[t], third[t]] for t in range(3)], shape)
     rest = [exchange(send[t], "dp", t) for t in range(3)]

time: 141 us -> 141 us (level)
  transfers between devices with their start and end apart: 24 -> 24, of which waited for: 12 -> 13; matrix products, arithmetic and copies ran while one was open for 0% -> 0% of each run, Pallas kernels for 24% -> 24%
where the time goes in v1:
time: 141 us; the launch traced here: 138 us
  Pallas kernels  58.3 us (41%)
  starting transfers between devices  40.4 us (29%)
  waiting for transfers between devices  36.5 us (26%)
  local copies, waits for them, and re-layouts  2.02 us (1%)
    ppermute x19, starting transfers between devices, exchange(): return lax.ppermute(x, axis, pairs)  37.3 us
    ppermute x19, waiting for transfers between devices, exchange(): return lax.ppermute(x, axis, pairs)  33.1 us
    pallas_call x1, Pallas kernels, chain_other(): pl.pallas_call(other_kernel, out_shape=jax.ShapeDtypeStruct((M, 864, 640)...  20.4 us
    pallas_call x1, Pallas kernels, chain_mine(): pl.pallas_call(mine_kernel, out_shape=jax.ShapeDtypeStruct((M, 864, 640),...  16.2 us
    pallas_call x4, Pallas kernels, route(): pl.pallas_call(functools.partial(route_kernel, chains, slots, count, part...  14 us
    pallas_call x1, Pallas kernels, pack(): pl.pallas_call(pack_kernel, out_shape=[jax.ShapeDtypeStruct((slots, PIECE...  3.63 us
    ppermute x3, waiting for transfers between devices, precondition(): lax.ppermute(x, 'fsdp', [(f, f ^ 1) for f in range(16)])  3.34 us
  transfers between devices with their start and end apart: 24, of which 13 were waited for; matrix products, arithmetic and copies ran while one was open for 0% of the time, Pallas kernels for 24%

profile of v1, /device:TPU:0, one launch (start us, length us, event | category | flops | bytes accessed | tf_op | source)
XLA Modules:
  0.0 138.3 jit_solution(10030631095662828631)
XLA Ops:
  0.0 1.7 %tables.1 = (s32[115]{0:T(128)S(1)}, s32[1]{0:T(128)}) custom-call(s32[2,3]{1,0:T(2,128)} %bitcast.22), custom_call_target="tpu_custom_call" | custom-call | tf_op jit(solution)/shard_map/tables/pallas_call | solution.py:102
  2.3 115.6 %conditional.1 = (f32[6,864,640]{2,1,0:T(8,128)}, f32[6,48,896]{2,1,0:T(8,128)}, f32[6,48,896]{2,1,0:T(8,128)}, f32[6,48,896]{2,1,0:T(8,128)}, f32[2,336,128]{2,...) conditional(s32[]{:T(128)} %bitcast.3, (s32[115]{0:T(128)S(1)}, ...), branch_computations={%region_0.0_spmd, %region_1.0_spmd, %region_2.0_spmd} | conditional | flops 1000000 | bytes 165379440 | solution.py:407
  2.4 2.5 %gather.3 = f32[2,336,128]{2,1,0:T(8,128)} custom-call(s32[115]{0:T(128)S(1)} %get-tuple-element.41.table_ref, f32[6,320,128]{2,1,0:T(8,128)} %get-tuple-element.69.basis_ref, f32[3,2,1,320]{3,2,1,0:T(1,128)} %get-tuple-element.70.eig_ref), custom_call_target="tpu_custom_call" | custom-call | bytes 800000 | tf_op jit(solution)/shard_map/cond/branch_0_fun/gather/pallas_call | solution.py:174
  4.9 1.6 %collective-permute-start.12 = (f32[2,336,128]{2,1,0:T(8,128)}, f32[2,336,128]{2,1,0:T(8,128)S(1)}, u32[]{:S(2)}, u32[]{:S(2)}) collective-permute-start(f32[2,336,128]{2,1,0:T(8,128)} %gather.3), channel_id=1, source_target_pairs={{0,0},{1,1},{2,2},{3,3},{4,4},{5,5},{6,6},{7,7},{8,8},{9,9},{10,10... | collective-permute-start | bytes 1032200 | tf_op jit(solution)/shard_map/cond/branch_0_fun/ppermute | solution.py:368
  6.5 3.6 %pack.3 = (f32[2,48,896]{2,1,0:T(8,128)}, f32[2,48,896]{2,1,0:T(8,128)}, f32[2,48,896]{2,1,0:T(8,128)}, f32[2,48,896]{2,1,0:T(8,128)}, f32[2,48,896]{2,1,0:T(8,128)}, /*index=5*/f32[2,48,896]{2,1,0:T(8,128)}) custom-call(s32[115]{0:T(128)S(1)} %get-tuple-element.41.table_ref, ...), custom_call_target="tpu_custom_call" | custom-call | bytes 4000000 | tf_op jit(solution)/shard_map/cond/branch_0_fun/pack/pallas_call | solution.py:135
  10.1 4.1 %collective-permute-start = (f32[2,48,896]{2,1,0:T(8,128)}, f32[2,48,896]{2,1,0:T(8,128)S(1)}, u32[]{:S(2)}, u32[]{:S(2)}) collective-permute-start(f32[2,48,896]{2,1,0:T(8,128)} %get-tuple-element.46), channel_id=1, source_target_pairs={{0,64},{16,80},{32,96},{48,112},{64,0},{80,16},{96,32},{112,48},{1... | collective-permute-start | bytes 1032200 | tf_op jit(solution)/shard_map/cond/branch_0_fun/ppermute | solution.py:352
  14.2 2.9 %collective-permute-start.1 = (f32[2,48,896]{2,1,0:T(8,128)}, f32[2,48,896]{2,1,0:T(8,128)S(1)}, u32[]{:S(2)}, u32[]{:S(2)}) collective-permute-start(f32[2,48,896]{2,1,0:T(8,128)} %get-tuple-element.47), channel_id=1, source_target_pairs={{0,16},{16,0},{32,48},{48,32},{64,80},{80,64},{96,112},{112,96},{1... | collective-permute-start | bytes 1032200 | tf_op jit(solution)/shard_map/cond/branch_0_fun/ppermute | solution.py:352
  17.1 4.1 %collective-permute-start.2 = (f32[2,48,896]{2,1,0:T(8,128)}, f32[2,48,896]{2,1,0:T(8,128)S(1)}, u32[]{:S(2)}, u32[]{:S(2)}) collective-permute-start(f32[2,48,896]{2,1,0:T(8,128)} %get-tuple-element.48), channel_id=1, source_target_pairs={{0,48},{16,32},{32,16},{48,0},{64,112},{80,96},{96,80},{112,64},{1... | collective-permute-start | bytes 1032200 | tf_op jit(solution)/shard_map/cond/branch_0_fun/ppermute | solution.py:352
  22.7 3.1 %collective-permute-done.refs_1_ = f32[2,48,896]{2,1,0:T(8,128)S(1)} collective-permute-done((f32[2,48,896]{2,1,0:T(8,128)}, f32[2,48,896]{2,1,0:T(8,128)S(1)}, u32[]{:S(2)}, u32[]{:S(2)}) %collective-permute-start) | collective-permute-done | bytes 344096 | tf_op jit(solution)/shard_map/cond/branch_0_fun/ppermute | solution.py:352
  26.9 3.6 %collective-permute-done.2.refs_9_.refs_11_ = f32[2,48,896]{2,1,0:T(8,128)S(1)} collective-permute-done((f32[2,48,896]{2,1,0:T(8,128)}, f32[2,48,896]{2,1,0:T(8,128)S(1)}, u32[]{:S(2)}, u32[]{:S(2)}) %collective-permute-start.2) | collective-permute-done | bytes 344096 | tf_op jit(solution)/shard_map/cond/branch_0_fun/ppermute | solution.py:352
  31.3 2.4 %collective-permute-done.3.refs_2_ = f32[2,48,896]{2,1,0:T(8,128)S(1)} collective-permute-done((f32[2,48,896]{2,1,0:T(8,128)}, f32[2,48,896]{2,1,0:T(8,128)S(1)}, u32[]{:S(2)}, u32[]{:S(2)}) %collective-permute-start.3) | collective-permute-done | bytes 344096 | tf_op jit(solution)/shard_map/cond/branch_0_fun/ppermute | solution.py:352
  33.7 5.6 %collective-permute-start.7 = (f32[2,48,896]{2,1,0:T(8,128)S(1)}, f32[2,48,896]{2,1,0:T(8,128)S(1)}, u32[]{:S(2)}, u32[]{:S(2)}) collective-permute-start(f32[2,48,896]{2,1,0:T(8,128)S(1)} %collective-permute-done.1.refs_5_.refs_6_), channel_id=1, source_target_pairs={{0,48},{16,32},{32,16},{48,0},{64,112},{80,96},{96,80},{112,64},{1... | collective-permute-start | bytes 1032200 | tf_op jit(solution)/shard_map/cond/branch_0_fun/ppermute | solution.py:352
  40.7 3.8 %collective-permute-done.7.refs_7_.refs_8_ = f32[2,48,896]{2,1,0:T(8,128)S(1)} collective-permute-done((f32[2,48,896]{2,1,0:T(8,128)S(1)}, f32[2,48,896]{2,1,0:T(8,128)S(1)}, u32[]{:S(2)}, u32[]{:S(2)}) %collective-permute-start.7) | collective-permute-done | bytes 344096 | tf_op jit(solution)/shard_map/cond/branch_0_fun/ppermute | solution.py:352
  44.5 4.8 %collective-permute-done.8.refs_11_.refs_13_ = f32[2,48,896]{2,1,0:T(8,128)} collective-permute-done((f32[2,48,896]{2,1,0:T(8,128)S(1)}, f32[2,48,896]{2,1,0:T(8,128)}, u32[]{:S(2)}, u32[]{:S(2)}) %collective-permute-start.8) | collective-permute-done | bytes 344096 | tf_op jit(solution)/shard_map/cond/branch_0_fun/ppermute | solution.py:352
  49.4 4.0 %route.12 = (f32[5,48,896]{2,1,0:T(8,128)}, f32[5,48,896]{2,1,0:T(8,128)}, f32[5,48,896]{2,1,0:T(8,128)}) custom-call(s32[115]{0:T(128)S(1)} %get-tuple-element.41.table_ref, f32[2,48,896]{2,1,0:T(8,128)} %get-tuple-element.45.refs_0_, f32[2,48,896]{2,1,0:T(8,128)} %copy-done.25, f32[2,48,896]{2,1,0:T(8,128)} %copy-done.28, f32[2,48,896]{2,1,0:T(8,128)} %copy-done.31, ...), custom_call_target="tpu_custom_call" | custom-call | bytes 2000000 | tf_op jit(solution)/shard_map/cond/branch_0_fun/route/pallas_call | solution.py:208
  53.4 3.6 %collective-permute-start.15 = (f32[2,336,128]{2,1,0:T(8,128)S(1)}, f32[2,336,128]{2,1,0:T(8,128)S(1)}, u32[]{:S(2)}, u32[]{:S(2)}) collective-permute-start(f32[2,336,128]{2,1,0:T(8,128)S(1)} %collective-permute-done.13.refs_0_), channel_id=1, source_target_pairs={{0,6},{1,7},{2,4},{3,5},{4,2},{5,3},{6,0},{7,1},{8,14},{9,15},{10,... | collective-permute-start | bytes 1032200 | tf_op jit(solution)/shard_map/cond/branch_0_fun/ppermute | solution.py:352
  57.0 2.1 %collective-permute-done.14.refs_1_ = f32[2,336,128]{2,1,0:T(8,128)S(1)} collective-permute-done((f32[2,336,128]{2,1,0:T(8,128)S(1)}, f32[2,336,128]{2,1,0:T(8,128)S(1)}, u32[]{:S(2)}, u32[]{:S(2)}) %collective-permute-start.14) | collective-permute-done | bytes 344096 | tf_op jit(solution)/shard_map/cond/branch_0_fun/ppermute | solution.py:352
  59.0 5.1 %collective-permute-start.16 = (f32[2,336,128]{2,1,0:T(8,128)S(1)}, f32[2,336,128]{2,1,0:T(8,128)S(1)}, u32[]{:S(2)}, u32[]{:S(2)}) collective-permute-start(f32[2,336,128]{2,1,0:T(8,128)S(1)} %collective-permute-done.14.refs_1_), channel_id=1, source_target_pairs={{0,6},{1,7},{2,4},{3,5},{4,2},{5,3},{6,0},{7,1},{8,14},{9,15},{10,... | collective-permute-start | bytes 1032200 | tf_op jit(solution)/shard_map/cond/branch_0_fun/ppermute | solution.py:352
  64.1 1.4 %collective-permute-start.9 = (f32[5,48,896]{2,1,0:T(8,128)}, f32[5,48,896]{2,1,0:T(8,128)S(1)}, u32[]{:S(2)}, u32[]{:S(2)}) collective-permute-start(f32[5,48,896]{2,1,0:T(8,128)} %get-tuple-element.60), channel_id=1, source_target_pairs={{0,48},{16,32},{32,16},{48,0},{64,112},{80,96},{96,80},{112,64},{1... | collective-permute-start | bytes 2580488 | tf_op jit(solution)/shard_map/cond/branch_0_fun/ppermute | solution.py:352
  65.5 1.4 %collective-permute-start.10 = (f32[5,48,896]{2,1,0:T(8,128)}, f32[5,48,896]{2,1,0:T(8,128)S(1)}, u32[]{:S(2)}, u32[]{:S(2)}) collective-permute-start(f32[5,48,896]{2,1,0:T(8,128)} %get-tuple-element.61), channel_id=1, source_target_pairs={{0,64},{16,80},{32,96},{48,112},{64,0},{80,16},{96,32},{112,48},{1... | collective-permute-start | bytes 2580488 | tf_op jit(solution)/shard_map/cond/branch_0_fun/ppermute | solution.py:352
  67.1 3.5 %collective-permute-done.16.refs_3_ = f32[2,336,128]{2,1,0:T(8,128)S(1)} collective-permute-done((f32[2,336,128]{2,1,0:T(8,128)S(1)}, f32[2,336,128]{2,1,0:T(8,128)S(1)}, u32[]{:S(2)}, u32[]{:S(2)}) %collective-permute-start.16) | collective-permute-done | bytes 344096 | tf_op jit(solution)/shard_map/cond/branch_0_fun/ppermute | solution.py:352
  71.4 2.8 %route.14 = f32[5,336,128]{2,1,0:T(8,128)} custom-call(s32[115]{0:T(128)S(1)} %get-tuple-element.41.table_ref, f32[2,336,128]{2,1,0:T(8,128)} %copy-done.21, f32[2,336,128]{2,1,0:T(8,128)} %copy-done.22, f32[2,336,128]{2,1,0:T(8,128)} %copy-done.23, f32[2,336,128]{2,1,0:T(8,128)} %copy-done.24), custom_call_target="tpu_custom_call" | custom-call | bytes 2000000 | tf_op jit(solution)/shard_map/cond/branch_0_fun/route/pallas_call | solution.py:208
  74.2 1.5 %collective-permute-start.17 = (f32[5,336,128]{2,1,0:T(8,128)}, f32[5,336,128]{2,1,0:T(8,128)S(1)}, u32[]{:S(2)}, u32[]{:S(2)}) collective-permute-start(f32[5,336,128]{2,1,0:T(8,128)} %route.14), channel_id=1, source_target_pairs={{0,2},{1,3},{2,0},{3,1},{4,6},{5,7},{6,4},{7,5},{8,10},{9,11},{10,... | collective-permute-start | bytes 2580488 | tf_op jit(solution)/shard_map/cond/branch_0_fun/ppermute | solution.py:352
  75.7 8.9 %collective-permute-done.9.refs_4_ = f32[5,48,896]{2,1,0:T(8,128)S(1)} collective-permute-done((f32[5,48,896]{2,1,0:T(8,128)}, f32[5,48,896]{2,1,0:T(8,128)S(1)}, u32[]{:S(2)}, u32[]{:S(2)}) %collective-permute-start.9) | collective-permute-done | bytes 860192 | tf_op jit(solution)/shard_map/cond/branch_0_fun/ppermute | solution.py:352
  85.8 4.3 %route.13 = (f32[6,48,896]{2,1,0:T(8,128)}, f32[6,48,896]{2,1,0:T(8,128)}, f32[6,48,896]{2,1,0:T(8,128)}) custom-call(s32[115]{0:T(128)S(1)} %get-tuple-element.41.table_ref, f32[2,48,896]{2,1,0:T(8,128)} %get-tuple-element.45.refs_0_, f32[2,48,896]{2,1,0:T(8,128)} %copy-done.25, f32[2,48,896]{2,1,0:T(8,128)} %copy-done.28, f32[2,48,896]{2,1,0:T(8,128)} %copy-done.31, ...), custom_call_target="tpu_custom_call" | custom-call | bytes 2400000 | tf_op jit(solution)/shard_map/cond/branch_0_fun/route/pallas_call | solution.py:208
  90.1 1.9 %collective-permute-start.21 = (f32[6,48,896]{2,1,0:T(8,128)}, f32[6,48,896]{2,1,0:T(8,128)}, u32[]{:S(2)}, u32[]{:S(2)}) collective-permute-start(f32[6,48,896]{2,1,0:T(8,128)} %get-tuple-element.66.p0), channel_id=1, source_target_pairs={{0,64},{16,80},{32,96},{48,112},{64,0},{80,16},{96,32},{112,48},{1... | collective-permute-start | bytes 3096584 | tf_op jit(solution)/shard_map/cond/branch_0_fun/ppermute | solution.py:352
  92.0 1.5 %collective-permute-start.23 = (f32[6,48,896]{2,1,0:T(8,128)}, f32[6,48,896]{2,1,0:T(8,128)}, u32[]{:S(2)}, u32[]{:S(2)}) collective-permute-start(f32[6,48,896]{2,1,0:T(8,128)} %get-tuple-element.68.p2), channel_id=1, source_target_pairs={{0,48},{16,32},{32,16},{48,0},{64,112},{80,96},{96,80},{112,64},{1... | collective-permute-start | bytes 3096584 | tf_op jit(solution)/shard_map/cond/branch_0_fun/ppermute | solution.py:352
  94.5 2.9 %route.15 = (f32[2,336,128]{2,1,0:T(8,128)}, f32[2,336,128]{2,1,0:T(8,128)}, f32[2,336,128]{2,1,0:T(8,128)}) custom-call(s32[115]{0:T(128)S(1)} %get-tuple-element.41.table_ref, f32[2,336,128]{2,1,0:T(8,128)} %copy-done.21, f32[2,336,128]{2,1,0:T(8,128)} %copy-done.22, f32[2,336,128]{2,1,0:T(8,128)} %copy-done.23, f32[2,336,128]{2,1,0:T(8,128)} %copy-done.24, ...), custom_call_target="tpu_custom_call" | custom-call | bytes 2400000 | tf_op jit(solution)/shard_map/cond/branch_0_fun/route/pallas_call | solution.py:208
  98.0 1.5 %collective-permute-done.18.refs_3_ = f32[2,336,128]{2,1,0:T(8,128)} collective-permute-done((f32[2,336,128]{2,1,0:T(8,128)}, f32[2,336,128]{2,1,0:T(8,128)}, u32[]{:S(2)}, u32[]{:S(2)}) %collective-permute-start.18) | collective-permute-done | bytes 344096 | tf_op jit(solution)/shard_map/cond/branch_0_fun/ppermute | solution.py:392
  100.0 1.5 %collective-permute-done.20.refs_5_ = f32[2,336,128]{2,1,0:T(8,128)} collective-permute-done((f32[2,336,128]{2,1,0:T(8,128)}, f32[2,336,128]{2,1,0:T(8,128)}, u32[]{:S(2)}, u32[]{:S(2)}) %collective-permute-start.20) | collective-permute-done | bytes 344096 | tf_op jit(solution)/shard_map/cond/branch_0_fun/ppermute | solution.py:392
  101.5 16.2 %mine.3 = f32[6,864,640]{2,1,0:T(8,128)} custom-call(s32[115]{0:T(128)S(1)} %get-tuple-element.41.table_ref, bf16[6,864,640]{2,1,0:T(8,128)(2,1)} %get-tuple-element.42.grad_ref, f32[6,48,896]{2,1,0:T(8,128)} %get-tuple-element.66.p0, f32[6,48,896]{2,1,0:T(8,128)} %get-tuple-element.67.p1, f32[6,48,896]{2,1,0:T(8,128)} %get-tuple-element.68.p2, ...), custom_call_target="tpu_custom_call" | custom-call | flops 1000000 | bytes 1000000 | tf_op jit(solution)/shard_map/cond/branch_0_fun/mine/pallas_call | solution.py:314
  118.0 20.4 %other.1 = bf16[6,864,640]{2,1,0:T(8,128)(2,1)} custom-call(s32[115]{0:T(128)S(1)} %get-tuple-element.158.table_ref, bf16[6,864,640]{2,1,0:T(8,128)(2,1)} %bitcast.18, f32[6,48,896]{2,1,0:T(8,128)} %get-tuple-element.160.p0, f32[6,48,896]{2,1,0:T(8,128)} %get-tuple-element.161.p1, f32[6,48,896]{2,1,0:T(8,128)} %get-tuple-element.162.p2, ...), custom_call_target="tpu_custom_call" | custom-call | flops 20000000000 | bytes 40000000 | tf_op jit(solution)/shard_map/other/pallas_call | solution.py:331
  (56 shorter events, 8.9 us)
Async XLA Ops:
  4.9 17.2 %collective-permute-start.12 = (f32[2,336,128]{2,1,0:T(8,128)}, f32[2,336,128]{2,1,0:T(8,128)S(1)}, u32[]{:S(2)}, u32[]{:S(2)}) collective-permute-start(f32[2,336,128]{2,1,0:T(8,128)} %gather.3), channel_id=1, source_target_pairs={{0,0},{1,1},{2,2},{3,3},{4,4},{5,5},{6,6},{7,7},{8,8},{9,9},{10,10... | collective-permute-start | bytes 1032200 | tf_op jit(solution)/shard_map/cond/branch_0_fun/ppermute | solution.py:368
  10.1 15.7 %collective-permute-start = (f32[2,48,896]{2,1,0:T(8,128)}, f32[2,48,896]{2,1,0:T(8,128)S(1)}, u32[]{:S(2)}, u32[]{:S(2)}) collective-permute-start(f32[2,48,896]{2,1,0:T(8,128)} %get-tuple-element.46), channel_id=1, source_target_pairs={{0,64},{16,80},{32,96},{48,112},{64,0},{80,16},{96,32},{112,48},{1... | collective-permute-start | bytes 1032200 | tf_op jit(solution)/shard_map/cond/branch_0_fun/ppermute | solution.py:352
  14.2 12.3 %collective-permute-start.1 = (f32[2,48,896]{2,1,0:T(8,128)}, f32[2,48,896]{2,1,0:T(8,128)S(1)}, u32[]{:S(2)}, u32[]{:S(2)}) collective-permute-start(f32[2,48,896]{2,1,0:T(8,128)} %get-tuple-element.47), channel_id=1, source_target_pairs={{0,16},{16,0},{32,48},{48,32},{64,80},{80,64},{96,112},{112,96},{1... | collective-permute-start | bytes 1032200 | tf_op jit(solution)/shard_map/cond/branch_0_fun/ppermute | solution.py:352
  17.1 13.3 %collective-permute-start.2 = (f32[2,48,896]{2,1,0:T(8,128)}, f32[2,48,896]{2,1,0:T(8,128)S(1)}, u32[]{:S(2)}, u32[]{:S(2)}) collective-permute-start(f32[2,48,896]{2,1,0:T(8,128)} %get-tuple-element.48), channel_id=1, source_target_pairs={{0,48},{16,32},{32,16},{48,0},{64,112},{80,96},{96,80},{112,64},{1... | collective-permute-start | bytes 1032200 | tf_op jit(solution)/shard_map/cond/branch_0_fun/ppermute | solution.py:352
  21.3 12.4 %collective-permute-start.3 = (f32[2,48,896]{2,1,0:T(8,128)}, f32[2,48,896]{2,1,0:T(8,128)S(1)}, u32[]{:S(2)}, u32[]{:S(2)}) collective-permute-start(f32[2,48,896]{2,1,0:T(8,128)} %get-tuple-element.45.refs_0_), channel_id=1, source_target_pairs={{0,16},{16,0},{32,48},{48,32},{64,80},{80,64},{96,112},{112,96},{1... | collective-permute-start | bytes 1032200 | tf_op jit(solution)/shard_map/cond/branch_0_fun/ppermute | solution.py:352
  22.1 17.2 %collective-permute-start.4 = (f32[2,48,896]{2,1,0:T(8,128)}, f32[2,48,896]{2,1,0:T(8,128)S(1)}, u32[]{:S(2)}, u32[]{:S(2)}) collective-permute-start(f32[2,48,896]{2,1,0:T(8,128)} %get-tuple-element.50.refs_4_.refs_5_), channel_id=1, source_target_pairs={{0,48},{16,32},{32,16},{48,0},{64,112},{80,96},{96,80},{112,64},{1... | collective-permute-start | bytes 1032200 | tf_op jit(solution)/shard_map/cond/branch_0_fun/ppermute | solution.py:352
  25.8 23.5 %copy-start.25 = (f32[2,48,896]{2,1,0:T(8,128)}, f32[2,48,896]{2,1,0:T(8,128)S(1)}, u32[]{:S(2)}) copy-start(f32[2,48,896]{2,1,0:T(8,128)S(1)} %collective-permute-done.refs_1_) | copy-start | bytes 1032196 | tf_op jit(solution)/shard_map/cond
  25.8 13.5 %collective-permute-start.13 = (f32[2,336,128]{2,1,0:T(8,128)S(1)}, f32[2,336,128]{2,1,0:T(8,128)S(1)}, u32[]{:S(2)}, u32[]{:S(2)}) collective-permute-start(f32[2,336,128]{2,1,0:T(8,128)S(1)} %collective-permute-done.12), channel_id=1, source_target_pairs={{0,0},{1,1},{2,18},{3,19},{4,36},{5,37},{6,54},{7,55},{8,72},{9,73... | collective-permute-start | bytes 1032200 | tf_op jit(solution)/shard_map/cond/branch_0_fun/ppermute | solution.py:369
  26.5 22.8 %copy-start.26 = (f32[2,48,896]{2,1,0:T(8,128)}, f32[2,48,896]{2,1,0:T(8,128)S(1)}, u32[]{:S(2)}) copy-start(f32[2,48,896]{2,1,0:T(8,128)S(1)} %collective-permute-done.1.refs_5_.refs_6_) | copy-start | bytes 1032196 | tf_op jit(solution)/shard_map/cond
  26.5 14.2 %collective-permute-start.5 = (f32[2,48,896]{2,1,0:T(8,128)}, f32[2,48,896]{2,1,0:T(8,128)S(1)}, u32[]{:S(2)}, u32[]{:S(2)}) collective-permute-start(f32[2,48,896]{2,1,0:T(8,128)} %get-tuple-element.51.refs_8_.refs_10_), channel_id=1, source_target_pairs={{0,64},{16,80},{32,96},{48,112},{64,0},{80,16},{96,32},{112,48},{1... | collective-permute-start | bytes 1032200 | tf_op jit(solution)/shard_map/cond/branch_0_fun/ppermute | solution.py:352
  30.5 18.9 %copy-start.27 = (f32[2,48,896]{2,1,0:T(8,128)}, f32[2,48,896]{2,1,0:T(8,128)S(1)}, u32[]{:S(2)}) copy-start(f32[2,48,896]{2,1,0:T(8,128)S(1)} %collective-permute-done.2.refs_9_.refs_11_) | copy-start | bytes 1032196 | tf_op jit(solution)/shard_map/cond
  30.5 10.3 %collective-permute-start.6 = (f32[2,48,896]{2,1,0:T(8,128)S(1)}, f32[2,48,896]{2,1,0:T(8,128)S(1)}, u32[]{:S(2)}, u32[]{:S(2)}) collective-permute-start(f32[2,48,896]{2,1,0:T(8,128)S(1)} %collective-permute-done.refs_1_), channel_id=1, source_target_pairs={{0,16},{16,0},{32,48},{48,32},{64,80},{80,64},{96,112},{112,96},{1... | collective-permute-start | bytes 1032200 | tf_op jit(solution)/shard_map/cond/branch_0_fun/ppermute | solution.py:352
  33.7 15.7 %copy-start.28 = (f32[2,48,896]{2,1,0:T(8,128)}, f32[2,48,896]{2,1,0:T(8,128)S(1)}, u32[]{:S(2)}) copy-start(f32[2,48,896]{2,1,0:T(8,128)S(1)} %collective-permute-done.3.refs_2_) | copy-start | bytes 1032196 | tf_op jit(solution)/shard_map/cond
  33.7 10.8 %collective-permute-start.7 = (f32[2,48,896]{2,1,0:T(8,128)S(1)}, f32[2,48,896]{2,1,0:T(8,128)S(1)}, u32[]{:S(2)}, u32[]{:S(2)}) collective-permute-start(f32[2,48,896]{2,1,0:T(8,128)S(1)} %collective-permute-done.1.refs_5_.refs_6_), channel_id=1, source_target_pairs={{0,48},{16,32},{32,16},{48,0},{64,112},{80,96},{96,80},{112,64},{1... | collective-permute-start | bytes 1032200 | tf_op jit(solution)/shard_map/cond/branch_0_fun/ppermute | solution.py:352
  39.3 10.1 %copy-start.29 = (f32[2,48,896]{2,1,0:T(8,128)}, f32[2,48,896]{2,1,0:T(8,128)S(1)}, u32[]{:S(2)}) copy-start(f32[2,48,896]{2,1,0:T(8,128)S(1)} %collective-permute-done.4.refs_6_.refs_7_) | copy-start | bytes 1032196 | tf_op jit(solution)/shard_map/cond
  39.3 10.1 %collective-permute-start.8 = (f32[2,48,896]{2,1,0:T(8,128)S(1)}, f32[2,48,896]{2,1,0:T(8,128)}, u32[]{:S(2)}, u32[]{:S(2)}) collective-permute-start(f32[2,48,896]{2,1,0:T(8,128)S(1)} %collective-permute-done.2.refs_9_.refs_11_), channel_id=1, source_target_pairs={{0,64},{16,80},{32,96},{48,112},{64,0},{80,16},{96,32},{112,48},{1... | collective-permute-start | bytes 1032200 | tf_op jit(solution)/shard_map/cond/branch_0_fun/ppermute | solution.py:352
  39.4 31.3 %copy-start.21 = (f32[2,336,128]{2,1,0:T(8,128)}, f32[2,336,128]{2,1,0:T(8,128)S(1)}, u32[]{:S(2)}) copy-start(f32[2,336,128]{2,1,0:T(8,128)S(1)} %collective-permute-done.13.refs_0_) | copy-start | bytes 1032196 | tf_op jit(solution)/shard_map/cond
  39.4 19.7 %collective-permute-start.14 = (f32[2,336,128]{2,1,0:T(8,128)S(1)}, f32[2,336,128]{2,1,0:T(8,128)S(1)}, u32[]{:S(2)}, u32[]{:S(2)}) collective-permute-start(f32[2,336,128]{2,1,0:T(8,128)S(1)} %collective-permute-done.13.refs_0_), channel_id=1, source_target_pairs={{0,8},{1,9},{2,10},{3,11},{4,12},{5,13},{6,14},{7,15},{8,0},{9,1},... | collective-permute-start | bytes 1032200 | tf_op jit(solution)/shard_map/cond/branch_0_fun/ppermute | solution.py:352
  40.7 8.7 %copy-start.31 = (f32[2,48,896]{2,1,0:T(8,128)}, f32[2,48,896]{2,1,0:T(8,128)S(1)}, u32[]{:S(2)}) copy-start(f32[2,48,896]{2,1,0:T(8,128)S(1)} %collective-permute-done.6.refs_3_) | copy-start | bytes 1032196 | tf_op jit(solution)/shard_map/cond
  53.4 13.7 %collective-permute-start.15 = (f32[2,336,128]{2,1,0:T(8,128)S(1)}, f32[2,336,128]{2,1,0:T(8,128)S(1)}, u32[]{:S(2)}, u32[]{:S(2)}) collective-permute-start(f32[2,336,128]{2,1,0:T(8,128)S(1)} %collective-permute-done.13.refs_0_), channel_id=1, source_target_pairs={{0,6},{1,7},{2,4},{3,5},{4,2},{5,3},{6,0},{7,1},{8,14},{9,15},{10,... | collective-permute-start | bytes 1032200 | tf_op jit(solution)/shard_map/cond/branch_0_fun/ppermute | solution.py:352
  59.0 11.7 %copy-start.22 = (f32[2,336,128]{2,1,0:T(8,128)}, f32[2,336,128]{2,1,0:T(8,128)S(1)}, u32[]{:S(2)}) copy-start(f32[2,336,128]{2,1,0:T(8,128)S(1)} %collective-permute-done.14.refs_1_) | copy-start | bytes 1032196 | tf_op jit(solution)/shard_map/cond
  59.0 11.6 %collective-permute-start.16 = (f32[2,336,128]{2,1,0:T(8,128)S(1)}, f32[2,336,128]{2,1,0:T(8,128)S(1)}, u32[]{:S(2)}, u32[]{:S(2)}) collective-permute-start(f32[2,336,128]{2,1,0:T(8,128)S(1)} %collective-permute-done.14.refs_1_), channel_id=1, source_target_pairs={{0,6},{1,7},{2,4},{3,5},{4,2},{5,3},{6,0},{7,1},{8,14},{9,15},{10,... | collective-permute-start | bytes 1032200 | tf_op jit(solution)/shard_map/cond/branch_0_fun/ppermute | solution.py:352
  64.1 20.5 %collective-permute-start.9 = (f32[5,48,896]{2,1,0:T(8,128)}, f32[5,48,896]{2,1,0:T(8,128)S(1)}, u32[]{:S(2)}, u32[]{:S(2)}) collective-permute-start(f32[5,48,896]{2,1,0:T(8,128)} %get-tuple-element.60), channel_id=1, source_target_pairs={{0,48},{16,32},{32,16},{48,0},{64,112},{80,96},{96,80},{112,64},{1... | collective-permute-start | bytes 2580488 | tf_op jit(solution)/shard_map/cond/branch_0_fun/ppermute | solution.py:352
  65.5 19.3 %collective-permute-start.10 = (f32[5,48,896]{2,1,0:T(8,128)}, f32[5,48,896]{2,1,0:T(8,128)S(1)}, u32[]{:S(2)}, u32[]{:S(2)}) collective-permute-start(f32[5,48,896]{2,1,0:T(8,128)} %get-tuple-element.61), channel_id=1, source_target_pairs={{0,64},{16,80},{32,96},{48,112},{64,0},{80,16},{96,32},{112,48},{1... | collective-permute-start | bytes 2580488 | tf_op jit(solution)/shard_map/cond/branch_0_fun/ppermute | solution.py:352
  66.9 18.6 %collective-permute-start.11 = (f32[5,48,896]{2,1,0:T(8,128)}, f32[5,48,896]{2,1,0:T(8,128)}, u32[]{:S(2)}, u32[]{:S(2)}) collective-permute-start(f32[5,48,896]{2,1,0:T(8,128)} %get-tuple-element.62), channel_id=1, source_target_pairs={{0,16},{16,0},{32,48},{48,32},{64,80},{80,64},{96,112},{112,96},{1... | collective-permute-start | bytes 2580488 | tf_op jit(solution)/shard_map/cond/branch_0_fun/ppermute | solution.py:352
  74.2 19.3 %collective-permute-start.17 = (f32[5,336,128]{2,1,0:T(8,128)}, f32[5,336,128]{2,1,0:T(8,128)S(1)}, u32[]{:S(2)}, u32[]{:S(2)}) collective-permute-start(f32[5,336,128]{2,1,0:T(8,128)} %route.14), channel_id=1, source_target_pairs={{0,2},{1,3},{2,0},{3,1},{4,6},{5,7},{6,4},{7,5},{8,10},{9,11},{10,... | collective-permute-start | bytes 2580488 | tf_op jit(solution)/shard_map/cond/branch_0_fun/ppermute | solution.py:352
  90.1 27.5 %collective-permute-start.21 = (f32[6,48,896]{2,1,0:T(8,128)}, f32[6,48,896]{2,1,0:T(8,128)}, u32[]{:S(2)}, u32[]{:S(2)}) collective-permute-start(f32[6,48,896]{2,1,0:T(8,128)} %get-tuple-element.66.p0), channel_id=1, source_target_pairs={{0,64},{16,80},{32,96},{48,112},{64,0},{80,16},{96,32},{112,48},{1... | collective-permute-start | bytes 3096584 | tf_op jit(solution)/shard_map/cond/branch_0_fun/ppermute | solution.py:352
  92.0 25.7 %collective-permute-start.22 = (f32[6,48,896]{2,1,0:T(8,128)}, f32[6,48,896]{2,1,0:T(8,128)}, u32[]{:S(2)}, u32[]{:S(2)}) collective-permute-start(f32[6,48,896]{2,1,0:T(8,128)} %get-tuple-element.67.p1), channel_id=1, source_target_pairs={{0,16},{16,0},{32,48},{48,32},{64,80},{80,64},{96,112},{112,96},{1... | collective-permute-start | bytes 3096584 | tf_op jit(solution)/shard_map/cond/branch_0_fun/ppermute | solution.py:352
  92.0 25.7 %collective-permute-start.23 = (f32[6,48,896]{2,1,0:T(8,128)}, f32[6,48,896]{2,1,0:T(8,128)}, u32[]{:S(2)}, u32[]{:S(2)}) collective-permute-start(f32[6,48,896]{2,1,0:T(8,128)} %get-tuple-element.68.p2), channel_id=1, source_target_pairs={{0,48},{16,32},{32,16},{48,0},{64,112},{80,96},{96,80},{112,64},{1... | collective-permute-start | bytes 3096584 | tf_op jit(solution)/shard_map/cond/branch_0_fun/ppermute | solution.py:352
  97.4 2.1 %collective-permute-start.18 = (f32[2,336,128]{2,1,0:T(8,128)}, f32[2,336,128]{2,1,0:T(8,128)}, u32[]{:S(2)}, u32[]{:S(2)}) collective-permute-start(f32[2,336,128]{2,1,0:T(8,128)} %get-tuple-element.174.refs_0_), channel_id=1, source_target_pairs={{0,1},{1,0},{2,3},{3,2},{4,5},{5,4},{6,7},{7,6},{8,9},{9,8},{10,11... | collective-permute-start | bytes 1032200 | tf_op jit(solution)/shard_map/cond/branch_0_fun/ppermute | solution.py:392
  97.5 2.5 %collective-permute-start.19 = (f32[2,336,128]{2,1,0:T(8,128)}, f32[2,336,128]{2,1,0:T(8,128)}, u32[]{:S(2)}, u32[]{:S(2)}) collective-permute-start(f32[2,336,128]{2,1,0:T(8,128)} %get-tuple-element.175.refs_1_), channel_id=1, source_target_pairs={{0,1},{1,0},{2,3},{3,2},{4,5},{5,4},{6,7},{7,6},{8,9},{9,8},{10,11... | collective-permute-start | bytes 1032200 | tf_op jit(solution)/shard_map/cond/branch_0_fun/ppermute | solution.py:392
  99.5 2.0 %collective-permute-start.20 = (f32[2,336,128]{2,1,0:T(8,128)}, f32[2,336,128]{2,1,0:T(8,128)}, u32[]{:S(2)}, u32[]{:S(2)}) collective-permute-start(f32[2,336,128]{2,1,0:T(8,128)} %get-tuple-element.176.refs_2_), channel_id=1, source_target_pairs={{0,1},{1,0},{2,3},{3,2},{4,5},{5,4},{6,7},{7,6},{8,9},{9,8},{10,11... | collective-permute-start | bytes 1032200 | tf_op jit(solution)/shard_map/cond/branch_0_fun/ppermute | solution.py:392
  (7 other events, 20.7 us)
